TPU v7x, 32 devices: a whole 2x2x4 slice. The times are simulated.
32 devices in a mesh: grp: 4 (over y, core), shard: 8 (over z, x).
Axes of the slice: x: 2, y: 2, z: 4, core: 2. Of those that a mesh axis runs over, the one named last changes fastest.
Arguments:
- entity_rows: float32 [8192, 400], P('shard'), may hold values from -6 to 6
- entity_first: float32 [8192, 400], P('shard'), may hold values from -1.9073486e-06 to 1.9073486e-06
- entity_second: float32 [8192, 400], P('shard'), may hold values from 1.8335413e-15 to 7.334165e-15
- relation_rows: float32 [6272, 400], P('shard'), may hold values from -6 to 6
- relation_first: float32 [6272, 400], P('shard'), may hold values from -2.3841858e-06 to 2.3841858e-06
- relation_second: float32 [6272, 400], P('shard'), may hold values from 2.2617834e-15 to 9.0471335e-15
- requests: int32 [32, 8, 40], P(('grp', 'shard')), may hold values from 0 to 1807, as said below
- head_slots: int32 [32768], P(('grp', 'shard')), may hold values from 0 to 311, as said below
- relation_slots: int32 [32768], P(('grp', 'shard')), may hold values from 32 to 319, as said below
- tail_slots: int32 [32768], P(('grp', 'shard')), may hold values from 0 to 311, as said below
- neg_offsets: int32 [32768, 16], P(('grp', 'shard')), may hold values from 0 to 127
- valid_counts: int32 [32], P(('grp', 'shard')), may hold values from 1 to 1024
Outputs:
- entity_new: float32 [8192, 400], P('shard')
- entity_moment_one: float32 [8192, 400], P('shard')
- entity_moment_two: float32 [8192, 400], P('shard')
- relation_new: float32 [6272, 400], P('shard')
- relation_moment_one: float32 [6272, 400], P('shard')
- relation_moment_two: float32 [6272, 400], P('shard')
- entity_low: bfloat16 [8192, 400], P('shard')
- relation_low: bfloat16 [6272, 400], P('shard')
- loss_sum: float32 [1], replicated
- pair_count: float32 [1], replicated
Inputs may be any that keep to these rules, and one draw needn't show every extreme that they name: Entries 0 to 31 of each requests[d, p] name entity rows (below 1024), entries 32 to 39 name relation rows (1024 plus a relation index); the distinct ones come first, and the remaining slots repeat the first entry of their kind; for each device, the slots of at least one owner are all distinct in each kind. `head_slots`: head slots name distinct entity slots (c below 32) of their owner. `relation_slots`: relation slots name distinct relation slots (c at least 32) of their owner. `tail_slots`: tail slots name distinct entity slots of their owner.
All inputs are finite; a program needn't handle non-finite values.
Results may differ from a plain program's by a relative error of at most 0.001.
Values sent between devices are 32-bit elements; how exact they have to be, the bound alone decides.
A program may use at most 128 MiB of HBM per device.

v0:
```python
import jax
import jax.numpy as jnp
from jax import lax
from jax.sharding import PartitionSpec as P

D = 400
CAP_E = 32
SEG = 128
NEG = 16
STEP = 10


MARGIN = 0.1
EPS_DIST = 1e-06
BETA_ONE = 0.9
BETA_TWO = 0.999
RATE = 0.5
DECAY = 0.01
EPS_ADAM = 1e-08
HIGH = lax.Precision.HIGHEST


def totals(loss_part, pair_part):
    return lax.psum((loss_part, pair_part), ("grp", "shard"))


def adamw(weight, moment_one, moment_two, gradient):
    moment_one = BETA_ONE * moment_one + (1.0 - BETA_ONE) * gradient
    moment_two = BETA_TWO * moment_two + (1.0 - BETA_TWO) * gradient * gradient
    fix_one = 1.0 - BETA_ONE**STEP
    fix_two = 1.0 - BETA_TWO**STEP
    direction = moment_one / fix_one / (jnp.sqrt(moment_two / fix_two) + EPS_ADAM)
    return (weight - RATE * (direction + DECAY * weight), moment_one, moment_two)


def per_device(
    entity_rows,
    entity_first,
    entity_second,
    relation_rows,
    relation_first,
    relation_second,
    requests,
    head_slots,
    relation_slots,
    tail_slots,
    neg_offsets,
    valid_counts,
):
    entity_count = entity_rows.shape[0]
    ids_in = lax.all_to_all(requests[0], "shard", split_axis=0, concat_axis=0, tiled=True)
    entity_ids = ids_in[:, :CAP_E]
    relation_ids = ids_in[:, CAP_E:] - entity_count
    served = jnp.concatenate([entity_rows[entity_ids], relation_rows[relation_ids]], axis=1)
    fetched = lax.all_to_all(served, "shard", split_axis=0, concat_axis=0, tiled=True)
    slot_total = fetched.shape[0] * fetched.shape[1]
    fetched = fetched.reshape(slot_total, D)
    edge_total = head_slots.shape[0]
    segments = edge_total // SEG
    valid = valid_counts[0]
    all_slots = jnp.concatenate([head_slots, relation_slots, tail_slots], axis=0)
    picked_rows = fetched[all_slots]
    anchor = picked_rows[:edge_total] + picked_rows[edge_total : 2 * edge_total]
    target = picked_rows[2 * edge_total :]
    offset_pos = anchor - target
    dist_pos = jnp.sqrt(jnp.sum(offset_pos * offset_pos, axis=1) + EPS_DIST)
    anchor_seg = anchor.reshape(segments, SEG, D)
    target_seg = target.reshape(segments, SEG, D)
    offsets_seg = neg_offsets.reshape(segments, SEG, NEG)
    positions = jnp.arange(SEG, dtype=jnp.int32)
    picks = (offsets_seg[:, :, :, None] == positions[None, None, None, :]).astype(jnp.float32)
    gram = jnp.einsum("sad,sbd->sab", anchor_seg, target_seg, precision=HIGH)
    anchor_sq = jnp.sum(anchor_seg * anchor_seg, axis=2)
    target_sq = jnp.sum(target_seg * target_seg, axis=2)
    square_all = anchor_sq[:, :, None] + target_sq[:, None, :] - 2.0 * gram
    square_neg = jnp.sum(square_all[:, :, None, :] * picks, axis=3).reshape(edge_total, NEG)
    dist_neg = jnp.sqrt(jnp.maximum(square_neg, 0.0) + EPS_DIST)
    edge_index = jnp.arange(edge_total, dtype=jnp.int32)
    neg_edge = edge_index[:, None] // SEG * SEG + neg_offsets
    valid_mask = (
        (edge_index[:, None] < valid) & (neg_edge < valid) & (neg_edge != edge_index[:, None])
    )
    weights = valid_mask.astype(jnp.float32)
    margins = MARGIN + dist_pos[:, None] - dist_neg
    loss_part = jnp.sum(jax.nn.softplus(margins) * weights)
    pair_part = jnp.sum(weights)
    loss_total, pair_total = totals(loss_part, pair_part)
    factor = 1.0 / pair_total
    slopes = jax.nn.sigmoid(margins) * weights * factor
    slope_pos = jnp.sum(slopes, axis=1)
    unit_pos = offset_pos / dist_pos[:, None]
    coeffs = (slopes / dist_neg).reshape(segments, SEG, NEG)
    pair_matrix = jnp.sum(coeffs[:, :, :, None] * picks, axis=2)
    row_total = jnp.sum(pair_matrix, axis=2)
    column_total = jnp.sum(pair_matrix, axis=1)
    pull_anchor = jnp.einsum("sab,sbd->sad", pair_matrix, target_seg, precision=HIGH)
    pull_target = jnp.einsum("sab,sad->sbd", pair_matrix, anchor_seg, precision=HIGH)
    neg_anchor = (pull_anchor - row_total[:, :, None] * anchor_seg).reshape(edge_total, D)
    neg_target = (pull_target - column_total[:, :, None] * target_seg).reshape(edge_total, D)
    grad_anchor = slope_pos[:, None] * unit_pos + neg_anchor
    grad_target = -slope_pos[:, None] * unit_pos + neg_target
    edge_grads = jnp.concatenate([grad_anchor, grad_anchor, grad_target], axis=0)
    slot_grads = jnp.zeros((slot_total, D), jnp.float32).at[all_slots].add(edge_grads)
    returned = lax.all_to_all(
        slot_grads.reshape(served.shape), "shard", split_axis=0, concat_axis=0, tiled=True
    )
    entity_grad = (
        jnp.zeros(entity_rows.shape, jnp.float32)
        .at[entity_ids.reshape(-1)]
        .add(returned[:, :CAP_E].reshape(-1, D))
    )
    relation_grad = (
        jnp.zeros(relation_rows.shape, jnp.float32)
        .at[relation_ids.reshape(-1)]
        .add(returned[:, CAP_E:].reshape(-1, D))
    )
    entity_sum, relation_sum = lax.psum((entity_grad, relation_grad), "grp")
    entity_new, entity_one, entity_two = adamw(entity_rows, entity_first, entity_second, entity_sum)
    relation_new, relation_one, relation_two = adamw(
        relation_rows, relation_first, relation_second, relation_sum
    )
    return (
        entity_new,
        entity_one,
        entity_two,
        relation_new,
        relation_one,
        relation_two,
        entity_new.astype(jnp.bfloat16),
        relation_new.astype(jnp.bfloat16),
        loss_total.reshape(1),
        pair_total.reshape(1),
    )


def solution(mesh):
    placed = (
        P("shard", None),
        P("shard", None),
        P("shard", None),
        P("shard", None),
        P("shard", None),
        P("shard", None),
        P(("grp", "shard"), None, None),
        P(("grp", "shard")),
        P(("grp", "shard")),
        P(("grp", "shard")),
        P(("grp", "shard"), None),
        P(("grp", "shard")),
    )
    return jax.shard_map(
        per_device,
        mesh=mesh,
        in_specs=placed,
        out_specs=(
            P("shard", None),
            P("shard", None),
            P("shard", None),
            P("shard", None),
            P("shard", None),
            P("shard", None),
            P("shard", None),
            P("shard", None),
            P(),
            P(),
        ),
        check_vma=False,
    )
```

profile of v0, /device:TPU:0, one launch (start us, length us, event | category | flops | bytes accessed | tf_op | source)
XLA Modules:
  0.0 292.5 jit_solution(15071946965620258194)
XLA Ops:
  7.2 7.3 %all-to-all-start = ((s32[8,1,40]{2,1,0:T(1,128)}), s32[8,1,40]{2,1,0:T(1,128)S(1)}, u32[]{:S(2)}, u32[]{:S(2)}) async-start(s32[8,1,40]{2,1,0:T(1,128)} %bitcast.59), calls=%async_computation | async-start | bytes 8192 | tf_op jit(solution)/shard_map/all_to_all | solution.py:51
  14.4 3.0 %copy.125 = f32[784,400]{1,0:T(8,128)} copy(f32[784,400]{0,1:T(8,128)} %param.15) | data formatting | bytes 2508800 | tf_op args[3]
  25.1 5.1 %all-to-all-start.1 = ((f32[8,40,400]{2,1,0:T(8,128)}), f32[8,40,400]{2,1,0:T(8,128)S(1)}, u32[]{:S(2)}, u32[]{:S(2)}) async-start(f32[8,40,400]{2,1,0:T(8,128)} %pad_maximum_fusion), calls=%async_computation.1 | async-start | bytes 1310720 | tf_op jit(solution)/shard_map/all_to_all | solution.py:55
  30.9 41.2 %psum.28 = f32[]{:T(128)} all-reduce(f32[]{:T(128)} %get-tuple-element.68), channel_id=1, replica_groups=mesh['grp'=4,'shard'=8] {'grp','shard'}, use_global_device_ids=true, to_apply=%region_5.6 | all-reduce | flops 1 | bytes 8 | tf_op jit(solution)/shard_map/psum | solution.py:24
  73.2 12.9 %gather_fusion.2 = f32[3072,400]{1,0:T(8,128)} fusion(f32[320,400]{1,0:T(8,128)S(1)} %bitcast.39, s32[3072]{0:T(1024)S(1)} %broadcast_clamp_fusion), kind=kCustom, calls=%fused_computation.2 | custom fusion | bytes 9842688 | tf_op jit(solution)/shard_map/gather | solution.py:62
  86.0 4.5 %multiply_reduce_fusion.2 = (f32[1024]{0:T(1024)S(1)}, f32[1024]{0:T(1024)S(1)}, f32[1024]{0:T(1024)S(1)}, f32[1024,400]{1,0:T(8,128)S(1)}, f32[1024,400]{1,0:T(8,128)}) fusion(f32[3072,400]{1,0:T(8,128)} %gather_fusion.2), kind=kLoop, calls=%fused_computation.24 | loop fusion | flops 3273728 | bytes 8204288 | tf_op jit(solution)/shard_map/reduce_sum | solution.py:66
  92.3 2.8 copy.130
  95.1 3.7 %fusion.8 = f32[8,128,128]{2,1,0:T(8,128)S(1)} fusion(f32[8,128,400]{2,1,0:T(8,128)S(1)} %bitcast.41, f32[8,128,400]{2,1,0:T(8,128)} %bitcast.44, f32[8,128]{1,0:T(8,128)S(1)} %bitcast.57, f32[8,128]{1,0:T(8,128)S(1)} %bitcast.58), kind=kOutput, calls=%fused_computation.34 | convolution fusion | flops 629538816 | bytes 3809280 | tf_op jit(solution)/shard_map/sad,sbd->sab/dot_general | solution.py:72
  98.7 5.1 %select_reduce_fusion.3 = f32[8,128,16]{2,1,0:T(8,128)S(1)} fusion(f32[8,128,128]{2,1,0:T(8,128)S(1)} %fusion.8, s32[8,128,16]{2,1,0:T(8,128)S(1)} %bitcast.46), kind=kLoop, calls=%fused_computation.9 | loop fusion | flops 6275072 | bytes 655360 | tf_op jit(solution)/shard_map/reduce_sum | solution.py:76
  105.9 17.4 %select_reduce_fusion.1 = (f32[8,128]{1,0:T(8,128)S(1)}, f32[8,128]{1,0:T(8,128)S(1)}, f32[8,128,128]{2,1,0:T(8,128)S(1)}) fusion(f32[8,128,16]{2,1,0:T(8,128)} %bitcast.48, s32[8,128,16]{2,1,0:T(8,128)S(1)} %bitcast.47), kind=kLoop, calls=%fused_computation.7 | loop fusion | flops 10352640 | bytes 663552 | tf_op jit(solution)/shard_map/reduce_sum | solution.py:94
  123.3 6.6 %multiply_subtract_fusion.2 = f32[8,128,400]{1,2,0:T(8,128)} fusion(f32[8,128,400]{1,2,0:T(8,128)} %copy.129, f32[8,128,128]{2,1,0:T(8,128)S(1)} %get-tuple-element.55, f32[8,128,400]{2,1,0:T(8,128)} %bitcast.45, f32[8,128]{1,0:T(8,128)S(1)} %get-tuple-element.53), kind=kOutput, calls=%fused_computation.29 | convolution fusion | flops 629964800 | bytes 5443584 | tf_op jit(solution)/shard_map/sab,sbd->sad/dot_general | solution.py:96
  129.9 2.8 copy.159
  132.7 6.0 %multiply_subtract_fusion.1 = f32[8,128,400]{1,2,0:T(8,128)} fusion(f32[8,128,400]{1,2,0:T(8,128)} %copy.130, f32[8,128,128]{2,1,0:T(8,128)S(1)} %get-tuple-element.55, f32[8,128,400]{2,1,0:T(8,128)S(1)} %bitcast.42, f32[8,128]{1,0:T(8,128)S(1)} %get-tuple-element.54), kind=kOutput, calls=%fused_computation.28 | convolution fusion | flops 629964800 | bytes 5443584 | tf_op jit(solution)/shard_map/sab,sad->sbd/dot_general | solution.py:97
  138.7 2.9 copy.162
  141.6 4.5 %bitcast_add_fusion.1 = (f32[1024,400]{1,0:T(8,128)}, f32[1024,400]{1,0:T(8,128)}) fusion(f32[8,128,400]{2,1,0:T(8,128)} %copy.159, f32[1024]{0:T(1024)S(1)} %get-tuple-element.57, f32[1024]{0:T(1024)S(1)} %get-tuple-element.77, f32[1024,400]{1,0:T(8,128)S(1)} %get-tuple-element.70, f32[3072,400]{1,0:T(8,128)} %gather_fusion.2, f32[8,128,400]{2,1,0:T(8,128)} %copy.162, ...), kind=kLoop, calls=%fused_computation.21 | loop fusion | flops 2457600 | bytes 9842688 | tf_op jit(solution)/shard_map/add | solution.py:100
  146.1 21.6 %scatter_custom_fusion = f32[320,400]{1,0:T(8,128)} fusion(s32[3072]{0:T(1024)S(1)} %bitcast.54, f32[1024,400]{1,0:T(8,128)} %get-tuple-element.72, f32[]{:T(128)} %constant.92, f32[1024,400]{1,0:T(8,128)} %get-tuple-element.71, f32[]{:T(128)} %constant.25.clone.1), kind=kCustom, calls=%fused_computation.11 | custom fusion | flops 3686400 | bytes 3788808 | tf_op jit(solution)/shard_map/scatter-add | solution.py:103
  167.7 5.5 %all-to-all-start.2 = ((f32[8,40,400]{2,1,0:T(8,128)}), f32[8,40,400]{2,1,0:T(8,128)S(1)}, u32[]{:S(2)}, u32[]{:S(2)}) async-start(f32[8,40,400]{2,1,0:T(8,128)} %bitcast.20), calls=%async_computation.2 | async-start | bytes 1310720 | tf_op jit(solution)/shard_map/all_to_all | solution.py:104
  173.4 15.6 %all-to-all-done.2 = f32[8,40,400]{2,1,0:T(8,128)S(1)} async-done(((f32[8,40,400]{2,1,0:T(8,128)}), f32[8,40,400]{2,1,0:T(8,128)S(1)}, u32[]{:S(2)}, u32[]{:S(2)}) %all-to-all-start.2) | async-done | bytes 512032 | tf_op jit(solution)/shard_map/all_to_all | solution.py:104
  197.4 3.2 %copy.144 = f32[784,400]{1,0:T(8,128)} copy(f32[784,400]{0,1:T(8,128)} %param.17) | data formatting | bytes 2508800 | tf_op args[5]
  200.5 39.2 %psum.31 = f32[1]{0:T(128)} all-reduce(f32[1]{0:T(128)} %bitcast.24), channel_id=1, replica_groups=mesh['grp'=4,'shard'=8] {'grp','shard'}, use_global_device_ids=true, to_apply=%region_16.17 | all-reduce | flops 1 | bytes 8 | tf_op jit(solution)/shard_map/psum | solution.py:24
  239.7 26.0 %all-reduce.3.cloned.1.call-done = (f32[1024,400]{0,1:T(8,128)}, f32[784,400]{1,0:T(8,128)}) async-done(((f32[1024,400]{0,1:T(8,128)}, f32[784,400]{1,0:T(8,128)}), (f32[1024,400]{0,1:T(8,128)}, f32[784,400]{1,0:T(8,128)})) %all-reduce.3.cloned.1.call-update) | async-done | bytes 2892816 | tf_op jit(solution)/shard_map/psum | solution.py:117
  265.7 5.3 %fusion.24 = (bf16[784,400]{1,0:T(8,128)(2,1)}, f32[784,400]{1,0:T(8,128)}, f32[784,400]{1,0:T(8,128)}, f32[784,400]{1,0:T(8,128)}) fusion(f32[784,400]{1,0:T(8,128)S(1)} %copy-done, f32[784,400]{1,0:T(8,128)} %get-tuple-element.59, f32[784,400]{1,0:T(8,128)S(1)} %copy.143, f32[784,400]{1,0:T(8,128)} %copy.144), kind=kLoop, calls=%fused_computation.75 | loop fusion | flops 5017600 | bytes 9408000 | tf_op jit(solution)/shard_map/convert_element_type | solution.py:130
  271.0 3.1 %copy.147 = f32[784,400]{0,1:T(8,128)} copy(f32[784,400]{1,0:T(8,128)} %get-tuple-element.61) | data formatting | bytes 2508800
  279.7 6.0 %fusion.26 = (bf16[1024,400]{0,1:T(8,128)(2,1)}, f32[1024,400]{0,1:T(8,128)}, f32[1024,400]{0,1:T(8,128)}, f32[1024,400]{0,1:T(8,128)}) fusion(f32[1024,400]{0,1:T(8,128)S(1)} %copy-done.1, f32[1024,400]{0,1:T(8,128)} %get-tuple-element.58, f32[1024,400]{0,1:T(8,128)} %param.13, f32[1024,400]{0,1:T(8,128)} %param.14), kind=kLoop, calls=%fused_computation.76 | loop fusion | flops 6553600 | bytes 12288000 | tf_op jit(solution)/shard_map/convert_element_type | solution.py:129
  (57 shorter events, 25.6 us)
Async XLA Ops:
  7.2 13.7 %all-to-all-start = ((s32[8,1,40]{2,1,0:T(1,128)}), s32[8,1,40]{2,1,0:T(1,128)S(1)}, u32[]{:S(2)}, u32[]{:S(2)}) async-start(s32[8,1,40]{2,1,0:T(1,128)} %bitcast.59), calls=%async_computation | async-start | bytes 8192 | tf_op jit(solution)/shard_map/all_to_all | solution.py:51
  24.2 6.1 %copy-start.5 = (s32[1024,16]{0,1:T(8,128)S(1)}, s32[1024,16]{0,1:T(8,128)}, u32[]{:S(2)}) copy-start(s32[1024,16]{0,1:T(8,128)} %param.22) | copy-start | bytes 196612
  24.2 48.9 %copy-start.6 = (s32[1024]{0:T(1024)S(1)}, s32[1024]{0:T(1024)}, u32[]{:S(2)}) copy-start(s32[1024]{0:T(1024)} %param.21) | copy-start | bytes 12292
  24.2 48.9 %copy-start.7 = (s32[1024]{0:T(1024)S(1)}, s32[1024]{0:T(1024)}, u32[]{:S(2)}) copy-start(s32[1024]{0:T(1024)} %param.20) | copy-start | bytes 12292
  24.2 48.9 %copy-start.8 = (s32[1024]{0:T(1024)S(1)}, s32[1024]{0:T(1024)}, u32[]{:S(2)}) copy-start(s32[1024]{0:T(1024)} %param.19) | copy-start | bytes 12292
  25.1 48.0 %all-to-all-start.1 = ((f32[8,40,400]{2,1,0:T(8,128)}), f32[8,40,400]{2,1,0:T(8,128)S(1)}, u32[]{:S(2)}, u32[]{:S(2)}) async-start(f32[8,40,400]{2,1,0:T(8,128)} %pad_maximum_fusion), calls=%async_computation.1 | async-start | bytes 1310720 | tf_op jit(solution)/shard_map/all_to_all | solution.py:55
  167.7 21.3 %all-to-all-start.2 = ((f32[8,40,400]{2,1,0:T(8,128)}), f32[8,40,400]{2,1,0:T(8,128)S(1)}, u32[]{:S(2)}, u32[]{:S(2)}) async-start(f32[8,40,400]{2,1,0:T(8,128)} %bitcast.20), calls=%async_computation.2 | async-start | bytes 1310720 | tf_op jit(solution)/shard_map/all_to_all | solution.py:104
  173.2 92.5 %all-reduce.3.cloned.1.call-start = ((), (), s32[]{:S(2)}) async-start(), calls=%async_computation.3 | async-start | bytes 6488064 | tf_op jit(solution)/shard_map/psum | solution.py:117
  195.5 1.4 copy-start.4
  197.4 68.4 %copy-start = (f32[784,400]{1,0:T(8,128)S(1)}, f32[784,400]{1,0:T(8,128)}, u32[]{:S(2)}) copy-start(f32[784,400]{1,0:T(8,128)} %copy.125) | copy-start | bytes 3763204
  271.0 3.2 %copy-start.3 = (f32[784,400]{1,0:T(8,128)S(1)}, f32[784,400]{1,0:T(8,128)}, u32[]{:S(2)}) copy-start(f32[784,400]{1,0:T(8,128)} %get-tuple-element.62) | copy-start | bytes 3763204
  274.1 1.6 copy-start.2
  275.8 3.9 %copy-start.1 = (f32[1024,400]{0,1:T(8,128)S(1)}, f32[1024,400]{0,1:T(8,128)}, u32[]{:S(2)}) copy-start(f32[1024,400]{0,1:T(8,128)} %param.12) | copy-start | bytes 4915204
Sparse Core Ops, SparseCore 0:
  195.6 70.0 all-reduce.2
where the time goes:
time: 293 us
  blocking collectives  80.5 us (27%)
  other arithmetic  71.7 us (24%)
  local copies, waits for them, and re-layouts  48.1 us (16%)
  waiting for transfers between devices  42.5 us (15%)
  starting transfers between devices  17.9 us (6%)
  matrix products  16.3 us (6%)
  between operations  15.6 us (5%)
    psum x2, blocking collectives, totals(): return lax.psum((loss_part, pair_part), ('grp', 'shard'))  80.5 us
    psum x1, waiting for transfers between devices, per_device(): entity_sum, relation_sum = lax.psum((entity_grad, relation_grad), 'grp')  26 us
    scatter-add x1, other arithmetic, per_device(): jnp.zeros((slot_total, D), jnp.float32).at[all_slots].add(edge_grads)  21.6 us
    unnamed x26, local copies, waits for them, and re-layouts  18.6 us
    reduce_sum x1, other arithmetic, per_device(): row_total = jnp.sum(pair_matrix, axis=2)  17.4 us
    all_to_all x1, waiting for transfers between devices, per_device(): lax.all_to_all(slot_grads.reshape(served.shape), 'shard', split_axis=0, c...  15.6 us
    gather x1, local copies, waits for them, and re-layouts, per_device(): picked_rows = fetched[all_slots]  12.9 us
    all_to_all x1, starting transfers between devices, per_device(): lax.all_to_all(requests[0], 'shard', split_axis=0, concat_axis=0, tiled=T...  7.26 us
  transfers between devices with their start and end apart: 4, of which 3 were waited for; matrix products, arithmetic and copies ran while one was open for 3% of the time, Pallas kernels for 0%

commit v1 on v0

v1 whole, which is shorter than its diff:
```python
import functools

import jax
import jax.numpy as jnp
from jax import lax
from jax.experimental import pallas as pl
from jax.experimental.pallas import tpu as pltpu
from jax.sharding import PartitionSpec as P

CAP_E = 32
SEG = 128
STEP = 10
LANE = 128

MARGIN = 0.1
EPS_DIST = 1e-06
BETA_ONE = 0.9
BETA_TWO = 0.999
RATE = 0.5
DECAY = 0.01
EPS_ADAM = 1e-08

F32 = jnp.float32
BF16 = jnp.bfloat16
I32 = jnp.int32


def mm(a, b):
    return lax.dot_general(a, b, (((1,), (0,)), ((), ())), preferred_element_type=F32)


def mm_nt(a, b):
    return lax.dot_general(a, b, (((1,), (1,)), ((), ())), preferred_element_type=F32)


def halves(x):
    hi = x.astype(BF16)
    return hi, (x - hi.astype(F32)).astype(BF16)


def up(n, m):
    return (n + m - 1) // m * m


def iota(shape, axis):
    return lax.broadcasted_iota(I32, shape, axis)


def far_first(n):
    return sorted(range(1, n), key=lambda k: (abs(k - n // 2), k))


def exchange_kernel(
    ns,
    ng,
    dims,
    valid_ref,
    ent_hbm,
    rel_hbm,
    req_hbm,
    head_hbm,
    rslot_hbm,
    tail_hbm,
    neg_hbm,
    ge_ref,
    gr_ref,
    stat_ref,
    ent_v,
    rel_v,
    req_v,
    slots_v,
    neg_v,
    eth,
    etl,
    rth,
    rtl,
    ids_all,
    idg,
    send_buf,
    recv_buf,
    rows_e,
    rows_r,
    oh_e,
    oh_r,
    hot_h,
    hot_t,
    hot_r,
    hott,
    hott_r,
    wt,
    eh,
    el,
    rr,
    gg_h,
    gg_l,
    gbuf,
    sgt_e,
    sgt_r,
    local_sem,
    ids_send,
    ids_recv,
    idg_send,
    idg_recv,
    f_send,
    f_recv,
    g_send,
    g_recv,
    core_send,
    y_send,
):
    d, ne, nr, cap, edges, neg = dims
    cap_r = cap - CAP_E
    ke, kr = ns * CAP_E, ns * cap_r
    chunks = d // LANE
    rest = d - chunks * LANE
    dp = (chunks + 1) * LANE
    nrp = up(nr, LANE)
    segs = edges // SEG
    copies = LANE // rest
    subs = cap // 8
    ny = ng // 2

    g = lax.axis_index("grp")
    s = lax.axis_index("shard")
    mate = g + 1 - 2 * lax.rem(g, 2)
    order = far_first(ns)

    def shard_at(k):
        return lax.rem(s + k, ns)

    def shard_from(k):
        return lax.rem(s + ns - k, ns)

    barrier = pltpu.get_barrier_semaphore()
    for k in range(1, ns):
        pl.semaphore_signal(barrier, inc=1, device_id={"shard": shard_at(k)})
    for k in range(1, ng):
        pl.semaphore_signal(barrier, inc=1, device_id={"grp": lax.rem(g + k, ng)})

    local = [
        pltpu.make_async_copy(src, dst, local_sem.at[i])
        for i, (src, dst) in enumerate(
            [
                (req_hbm, req_v),
                (ent_hbm, ent_v),
                (rel_hbm, rel_v),
                (head_hbm, slots_v.at[0]),
                (rslot_hbm, slots_v.at[1]),
                (tail_hbm, slots_v.at[2]),
                (neg_hbm, neg_v),
            ]
        )
    ]
    for copy in local:
        copy.start()
    local[0].wait()
    pl.semaphore_wait(barrier, ns - 1 + ng - 1)

    def ids_copy(k):
        return pltpu.make_async_remote_copy(
            src_ref=req_v,
            dst_ref=ids_all.at[s],
            send_sem=ids_send.at[k],
            recv_sem=ids_recv.at[s],
            device_id={"shard": shard_at(k)},
        )

    def ids_arrival(k):
        return pltpu.make_async_remote_copy(
            src_ref=req_v,
            dst_ref=ids_all.at[shard_from(k)],
            send_sem=ids_send.at[k],
            recv_sem=ids_recv.at[shard_from(k)],
            device_id={"shard": shard_from(k)},
        )

    for k in order:
        ids_copy(k).start()
    ids_all[s] = req_v[...]

    local[1].wait()
    local[2].wait()

    def split_rows(i, _):
        at = pl.ds(pl.multiple_of(i * 16, 16), 16)
        hi, lo = halves(ent_v[at, :])
        eth[at, :] = hi
        etl[at, :] = lo
        hi, lo = halves(rel_v[at, :])
        rth[at, 0:nr] = hi
        rtl[at, 0:nr] = lo
        return 0

    if nrp > nr:
        rth[:, nr:nrp] = jnp.zeros((dp, nrp - nr), BF16)
        rtl[:, nr:nrp] = jnp.zeros((dp, nrp - nr), BF16)
    lax.fori_loop(0, d // 16, split_rows, 0)
    for table in (eth, etl, rth, rtl):
        tail_rows = table[chunks * LANE : d, :]
        for c in range(1, copies):
            table[chunks * LANE + c * rest : chunks * LANE + (c + 1) * rest, :] = tail_rows

    for k in order:
        ids_arrival(k).wait_recv()
    for r in range(ns):
        idg[g, r : r + 1, :] = ids_all[r, pl.ds(s, 1), :]

    def idg_copy(k):
        return pltpu.make_async_remote_copy(
            src_ref=idg.at[g],
            dst_ref=idg.at[g],
            send_sem=idg_send.at[k],
            recv_sem=idg_recv.at[g],
            device_id={"grp": lax.rem(g + k, ng)},
        )

    def idg_arrival(k):
        other = lax.rem(g + ng - k, ng)
        return pltpu.make_async_remote_copy(
            src_ref=idg.at[other],
            dst_ref=idg.at[other],
            send_sem=idg_send.at[k],
            recv_sem=idg_recv.at[other],
            device_id={"grp": other},
        )

    def one_hots(grp):
        wide = jnp.concatenate([idg[grp].astype(F32), jnp.zeros((ns, LANE - cap), F32)], axis=1)
        columns = jnp.concatenate([wide] + [jnp.zeros((LANE - ns, LANE), F32)], axis=0).T
        lanes_e = iota((CAP_E, ne), 1).astype(F32)
        lanes_r = iota((cap_r, nrp), 1).astype(F32) + float(ne)
        pieces = []
        for r in range(ns):
            column = columns[:, r : r + 1]
            hit = jnp.where(column[0:CAP_E] == lanes_e, 1.0, 0.0).astype(BF16)
            oh_e[r * CAP_E : (r + 1) * CAP_E, :] = hit
            pieces.append(jnp.where(column[CAP_E:cap] == lanes_r, 1.0, 0.0))
        for r in range(0, ns, 2):
            oh_r[r * cap_r : (r + 2) * cap_r, :] = jnp.concatenate(pieces[r : r + 2], axis=0).astype(BF16)

    one_hots(g)
    rows_e[...] = mm_nt(oh_e[...], eth[...]) + mm_nt(oh_e[...], etl[...])
    rows_r[...] = mm_nt(oh_r[...], rth[...]) + mm_nt(oh_r[...], rtl[...])

    lane8 = iota((8, LANE), 1)

    def pack(r, roll, extra):
        for c in range(chunks):
            at = slice(c * LANE, (c + 1) * LANE)
            send_buf[r, c * cap : c * cap + CAP_E, :] = rows_e[r * CAP_E : (r + 1) * CAP_E, at]
            send_buf[r, c * cap + CAP_E : (c + 1) * cap, :] = rows_r[r * cap_r : (r + 1) * cap_r, at]
        last = slice(chunks * LANE, dp)
        out = extra
        for j in range(subs):
            if j * 8 < CAP_E:
                piece = rows_e[r * CAP_E + j * 8 : r * CAP_E + j * 8 + 8, last]
            else:
                piece = rows_r[r * cap_r + j * 8 - CAP_E : r * cap_r + j * 8 - CAP_E + 8, last]
            if roll and j:
                piece = pltpu.roll(piece, j * rest, 1)
            out = jnp.where((lane8 >= j * rest) & (lane8 < (j + 1) * rest), piece, out)
        send_buf[r, chunks * cap : chunks * cap + 8, :] = out

    def last_columns(tile):
        pieces = []
        for j in range(subs):
            piece = pltpu.roll(tile, LANE - j * rest, 1) if j else tile
            pieces.append(jnp.where(lane8 < rest, piece, 0.0))
        return jnp.concatenate(pieces[: CAP_E // 8], axis=0), jnp.concatenate(pieces[CAP_E // 8 :], axis=0)

    def fetch_copy(k):
        peer = shard_at(k)
        return pltpu.make_async_remote_copy(
            src_ref=send_buf.at[peer],
            dst_ref=recv_buf.at[s],
            send_sem=f_send.at[k],
            recv_sem=f_recv.at[s],
            device_id={"shard": peer},
        )

    def fetch_arrival(k):
        peer = shard_from(k)
        return pltpu.make_async_remote_copy(
            src_ref=send_buf.at[peer],
            dst_ref=recv_buf.at[peer],
            send_sem=f_send.at[k],
            recv_sem=f_recv.at[peer],
            device_id={"shard": peer},
        )

    for r in range(ns):
        pack(r, False, jnp.zeros((8, LANE), F32))
    for k in order:
        fetch_copy(k).start()
    recv_buf[s] = send_buf[s]
    for k in range(1, ng):
        idg_copy(k).start()

    for copy in local[3:]:
        copy.wait()
    slots = slots_v[...]
    owner = lax.shift_right_logical(slots * ((1 << 16) // cap + 1), 16)
    within = slots - owner * cap
    head_k = owner[0] * CAP_E + within[0]
    rel_k = owner[1] * cap_r + within[1] - CAP_E
    tail_k = owner[2] * CAP_E + within[2]
    for i in range(segs):
        at = slice(i * SEG, (i + 1) * SEG)
        head_row, rel_row, tail_row = (v[i : i + 1, :] for v in (head_k, rel_k, tail_k))
        hott[:, at] = jnp.where(iota((ke, SEG), 0) == head_row, 1.0, 0.0).astype(BF16)
        hott[:, edges + i * SEG : edges + (i + 1) * SEG] = jnp.where(
            iota((ke, SEG), 0) == tail_row, 1.0, 0.0
        ).astype(BF16)
        hott_r[:, at] = jnp.where(iota((kr, SEG), 0) == rel_row, 1.0, 0.0).astype(BF16)
        head_col, rel_col, tail_col = (
            jnp.broadcast_to(v.astype(F32), (SEG, SEG)).T[:, 0:1] for v in (head_row, rel_row, tail_row)
        )
        lanes_e = iota((SEG, ke), 1).astype(F32)
        lanes_r = iota((SEG, kr), 1).astype(F32)
        hot_h[at, :] = jnp.where(lanes_e == head_col, 1.0, 0.0).astype(BF16)
        hot_t[at, :] = jnp.where(lanes_e == tail_col, 1.0, 0.0).astype(BF16)
        hit = jnp.where(lanes_r == rel_col, 1.0, 0.0)
        hot_r[at, :] = jnp.concatenate([hit, hit], axis=1).astype(BF16)

    valid = valid_ref[0]
    sub = iota((SEG, SEG), 0)
    lane = iota((SEG, SEG), 1)

    def count(i, total):
        start = pl.multiple_of(i * SEG, SEG)
        hits = jnp.zeros((SEG, SEG), F32)
        for k in range(neg):
            hits += jnp.where(neg_v[k : k + 1, pl.ds(start, SEG)] == sub, 1.0, 0.0)
        keep = (lane + start < valid) & (sub + start < valid) & (sub != lane)
        hits = jnp.where(keep, hits, 0.0)
        wt[i] = hits
        return total + hits

    pairs = jnp.sum(lax.fori_loop(0, segs, count, jnp.zeros((SEG, SEG), F32)))

    recv = [(s, None)] + [(shard_from(k), k) for k in order]
    for src, k in recv:
        if k is not None:
            fetch_arrival(k).wait_recv()
    for p in range(ns):
        ends_e, ends_r = last_columns(recv_buf[p, chunks * cap : chunks * cap + 8, :])
        e = jnp.concatenate(
            [recv_buf[p, c * cap : c * cap + CAP_E, :] for c in range(chunks)] + [ends_e], axis=1
        )
        r = jnp.concatenate(
            [recv_buf[p, c * cap + CAP_E : (c + 1) * cap, :] for c in range(chunks)] + [ends_r], axis=1
        )
        at = slice(p * CAP_E, (p + 1) * CAP_E)
        eh[at, :], el[at, :] = halves(e)
        rows_r[p * cap_r : (p + 1) * cap_r, :] = r
    hi, lo = halves(rows_r[...])
    rr[0:kr, :] = hi
    rr[kr : 2 * kr, :] = lo

    def lane_fold(x):
        out = x[:, 0:LANE]
        for c in range(1, dp // LANE):
            out += x[:, c * LANE : (c + 1) * LANE]
        return out

    def edge_step(i, loss):
        at = pl.ds(pl.multiple_of(i * SEG, SEG), SEG)
        at_t = pl.ds(pl.multiple_of(edges + i * SEG, SEG), SEG)
        a = mm(hot_h[at, :], eh[...]) + mm(hot_h[at, :], el[...]) + mm(hot_r[at, :], rr[...])
        t = mm(hot_t[at, :], eh[...]) + mm(hot_t[at, :], el[...])
        ah, al = halves(a)
        th, tl = halves(t)
        aa = jnp.concatenate([ah, al], axis=0)
        tt = jnp.concatenate([th, tl], axis=0)
        offset = a - t
        dist_pos = jnp.sqrt(jnp.sum(lane_fold(offset * offset).T, axis=0, keepdims=True) + EPS_DIST)
        anchor_sq = jnp.sum(lane_fold(a * a).T, axis=0, keepdims=True)
        target_sq = jnp.sum(lane_fold(t * t), axis=1, keepdims=True)
        near = mm_nt(th, aa)
        far = mm_nt(tl, aa)
        gram = near[:, 0:SEG] + (near[:, SEG:] + far[:, 0:SEG] + far[:, SEG:])
        square = jnp.maximum(anchor_sq + target_sq - 2.0 * gram, 0.0) + EPS_DIST
        inv = lax.rsqrt(square)
        m = MARGIN + dist_pos - square * inv
        w = wt[i]
        small = jnp.exp(-jnp.abs(m))
        loss += w * (jnp.maximum(m, 0.0) + jnp.log1p(small))
        slope = w * (jnp.where(m >= 0.0, 1.0, small) / (1.0 + small))
        ratio = jnp.sum(slope, axis=0, keepdims=True) / dist_pos
        pt = slope * inv - jnp.where(sub == lane, ratio, 0.0)
        pa = pt.T
        row_t = jnp.sum(pt, axis=1, keepdims=True)
        row_a = jnp.sum(pa, axis=1, keepdims=True)
        pth, ptl = halves(pt)
        pah, pal = halves(pa)
        grad_t = mm(jnp.concatenate([pth, pth], axis=1), aa) + mm(ptl, ah) - row_t * t
        grad_a = mm(jnp.concatenate([pah, pah], axis=1), tt) + mm(pal, th) - row_a * a
        gg_h[at, :], gg_l[at, :] = halves(grad_a)
        gg_h[at_t, :], gg_l[at_t, :] = halves(grad_t)
        return loss

    loss = jnp.sum(lax.fori_loop(0, segs, edge_step, jnp.zeros((SEG, SEG), F32)))

    rows_e[...] = mm(hott[...], gg_h[...]) + mm(hott[...], gg_l[...])
    rows_r[...] = mm(hott_r[...], gg_h[0:edges, :]) + mm(hott_r[...], gg_l[0:edges, :])
    at_loss = copies * rest - 2
    extra = jnp.where(lane8 == at_loss, loss, jnp.where(lane8 == at_loss + 1, pairs, 0.0))

    def grad_copy(k):
        peer = shard_at(k)
        return pltpu.make_async_remote_copy(
            src_ref=send_buf.at[peer],
            dst_ref=gbuf.at[g, s],
            send_sem=g_send.at[k],
            recv_sem=g_recv.at[g, s],
            device_id={"shard": peer},
        )

    def block_copy(grp, src, to, send_sem):
        return pltpu.make_async_remote_copy(
            src_ref=gbuf.at[grp, src],
            dst_ref=gbuf.at[grp, src],
            send_sem=send_sem,
            recv_sem=g_recv.at[grp, src],
            device_id={"grp": to},
        )

    def arrived(grp, src):
        block_copy(grp, src, mate, core_send.at[0, 0]).wait_recv()

    for k in order:
        fetch_copy(k).wait_send()
    for r in range(ns):
        pack(r, True, extra)
    for k in order:
        grad_copy(k).start()
    gbuf[g, s] = send_buf[s]

    def group_up(dy):
        return lax.rem(g + 2 * dy, ng)

    def group_down(dy):
        return lax.rem(g + ng - 2 * dy, ng)

    def forward(src):
        out = [block_copy(g, src, mate, core_send.at[0, src])]
        for dy in range(1, ny):
            out.append(block_copy(g, src, group_up(dy), y_send.at[dy - 1, src]))
        return out

    def hand_over(dy, src):
        return block_copy(group_down(dy), src, mate, core_send.at[dy, src])

    sequence = [0] + order
    lag = 2

    def hand_over_all(idx):
        src = shard_from(sequence[idx])
        for dy in range(1, ny):
            arrived(group_down(dy), src)
            hand_over(dy, src).start()

    for idx, k in enumerate(sequence):
        src = shard_from(k)
        if k:
            arrived(g, src)
        for copy in forward(src):
            copy.start()
        if idx >= lag:
            hand_over_all(idx - lag)

    def gather_blocks(grp):
        for r in range(ns):
            ends_e, ends_r = last_columns(gbuf[grp, r, chunks * cap : chunks * cap + 8, :])
            rows_e[r * CAP_E : (r + 1) * CAP_E, chunks * LANE : dp] = ends_e
            rows_r[r * cap_r : (r + 1) * cap_r, chunks * LANE : dp] = ends_r
            for c in range(chunks):
                at = slice(c * LANE, (c + 1) * LANE)
                rows_e[r * CAP_E : (r + 1) * CAP_E, at] = gbuf[grp, r, c * cap : c * cap + CAP_E, :]
                rows_r[r * cap_r : (r + 1) * cap_r, at] = gbuf[grp, r, c * cap + CAP_E : (c + 1) * cap, :]
        for c in range(chunks + 1):
            at = slice(c * LANE, (c + 1) * LANE)
            size = LANE if c < chunks else rest
            put = slice(c * LANE, c * LANE + size)
            hi, lo = halves(rows_e[:, at].T[0:size, :])
            sgt_e[put, 0:ke] = hi
            sgt_e[put, ke : 2 * ke] = lo
            hi, lo = halves(rows_r[:, at].T[0:size, :])
            sgt_r[put, 0:kr] = hi
            sgt_r[put, kr : 2 * kr] = lo

    def add_group(grp, first):
        gather_blocks(grp)
        part_e = mm(sgt_e[:, 0:ke], oh_e[...]) + mm(sgt_e[:, ke : 2 * ke], oh_e[...])
        part_r = mm(sgt_r[:, 0:kr], oh_r[...]) + mm(sgt_r[:, kr : 2 * kr], oh_r[...])
        if first:
            ge_ref[...] = part_e
            gr_ref[...] = part_r[:, 0:nr]
        else:
            ge_ref[...] += part_e
            gr_ref[...] += part_r[:, 0:nr]

    one_hots(g)
    add_group(g, True)
    for idx in range(max(len(sequence) - lag, 0), len(sequence)):
        hand_over_all(idx)
    for k in range(1, ng):
        idg_arrival(k).wait_recv()
    one_hots(mate)
    for k in sequence:
        arrived(mate, shard_from(k))
    add_group(mate, False)
    for dy in range(1, ny):
        one_hots(group_down(dy))
        add_group(group_down(dy), False)
        other = lax.rem(mate + ng - 2 * dy, ng)
        one_hots(other)
        for k in sequence:
            arrived(other, shard_from(k))
        add_group(other, False)

    def stat(i, total):
        for r in range(ns):
            total += gbuf[i, r, chunks * cap : chunks * cap + 8, :]
        return total

    stat_ref[...] = lax.fori_loop(0, ng, stat, jnp.zeros((8, LANE), F32))

    for k in order:
        ids_copy(k).wait_send()
        grad_copy(k).wait_send()
    for k in range(1, ng):
        idg_copy(k).wait_send()
    for k in sequence:
        src = shard_from(k)
        for copy in forward(src):
            copy.wait_send()
        for dy in range(1, ny):
            hand_over(dy, src).wait_send()


def adamw_kernel(at_pairs, stat_ref, *refs):
    factor = 1.0 / stat_ref[0:1, at_pairs : at_pairs + 1]
    fix_one = 1.0 - BETA_ONE**STEP
    fix_two = 1.0 - BETA_TWO**STEP
    for i in range(2):
        g_ref, w_ref, one_ref, two_ref = refs[4 * i : 4 * i + 4]
        w_out, one_out, two_out, low_out = refs[8 + 4 * i : 12 + 4 * i]
        gradient = g_ref[...] * factor
        weight = w_ref[...]
        one = BETA_ONE * one_ref[...] + (1.0 - BETA_ONE) * gradient
        two = BETA_TWO * two_ref[...] + (1.0 - BETA_TWO) * gradient * gradient
        direction = one / fix_one / (jnp.sqrt(two / fix_two) + EPS_ADAM)
        new = weight - RATE * (direction + DECAY * weight)
        w_out[...] = new
        one_out[...] = one
        two_out[...] = two
        low_out[...] = new.astype(BF16)


def per_device(
    ns,
    ng,
    entity_rows,
    entity_first,
    entity_second,
    relation_rows,
    relation_first,
    relation_second,
    requests,
    head_slots,
    relation_slots,
    tail_slots,
    neg_offsets,
    valid_counts,
):
    ne, d = entity_rows.shape
    nr = relation_rows.shape[0]
    cap = requests.shape[2]
    cap_r = cap - CAP_E
    edges, neg = neg_offsets.shape
    segs = edges // SEG
    ke, kr = ns * CAP_E, ns * cap_r
    chunks = d // LANE
    rest = d - chunks * LANE
    dp = (chunks + 1) * LANE
    nrp = up(nr, LANE)
    ny = ng // 2
    block = (LANE, LANE)
    any_space = pl.BlockSpec(memory_space=pl.ANY)
    vmem = pl.BlockSpec(memory_space=pltpu.VMEM)
    smem = pl.BlockSpec(memory_space=pltpu.SMEM)
    dma = pltpu.SemaphoreType.DMA
    ge, gr, stat = pl.pallas_call(
        functools.partial(exchange_kernel, ns, ng, (d, ne, nr, cap, edges, neg)),
        out_shape=(
            jax.ShapeDtypeStruct((d, ne), F32),
            jax.ShapeDtypeStruct((d, nr), F32),
            jax.ShapeDtypeStruct((8, LANE), F32),
        ),
        in_specs=[smem] + [any_space] * 7,
        out_specs=(vmem, vmem, vmem),
        scratch_shapes=[
            pltpu.VMEM((d, ne), F32),
            pltpu.VMEM((d, nr), F32),
            pltpu.VMEM((ns, cap), I32),
            pltpu.VMEM((3, segs, SEG), I32),
            pltpu.VMEM((neg, edges), I32),
            pltpu.VMEM((dp, ne), BF16),
            pltpu.VMEM((dp, ne), BF16),
            pltpu.VMEM((dp, nrp), BF16),
            pltpu.VMEM((dp, nrp), BF16),
            pltpu.VMEM((ns, ns, cap), I32),
            pltpu.VMEM((ng, ns, cap), I32),
            pltpu.VMEM((ns, *block), F32),
            pltpu.VMEM((ns, *block), F32),
            pltpu.VMEM((ke, dp), F32),
            pltpu.VMEM((kr, dp), F32),
            pltpu.VMEM((ke, ne), BF16),
            pltpu.VMEM((kr, nrp), BF16),
            pltpu.VMEM((edges, ke), BF16),
            pltpu.VMEM((edges, ke), BF16),
            pltpu.VMEM((edges, 2 * kr), BF16),
            pltpu.VMEM((ke, 2 * edges), BF16),
            pltpu.VMEM((kr, edges), BF16),
            pltpu.VMEM((segs, SEG, SEG), F32),
            pltpu.VMEM((ke, dp), BF16),
            pltpu.VMEM((ke, dp), BF16),
            pltpu.VMEM((2 * kr, dp), BF16),
            pltpu.VMEM((2 * edges, dp), BF16),
            pltpu.VMEM((2 * edges, dp), BF16),
            pltpu.VMEM((ng, ns, *block), F32),
            pltpu.VMEM((d, 2 * ke), BF16),
            pltpu.VMEM((d, 2 * kr), BF16),
            dma((7,)),
            dma((ns,)),
            dma((ns,)),
            dma((ng,)),
            dma((ng,)),
            dma((ns,)),
            dma((ns,)),
            dma((ns,)),
            dma((ng, ns)),
            dma((ny, ns)),
            dma((max(ny - 1, 1), ns)),
        ],
        compiler_params=pltpu.CompilerParams(
            collective_id=0, has_side_effects=True, vmem_limit_bytes=60 * 1024 * 1024
        ),
    )(
        valid_counts,
        entity_rows.T,
        relation_rows.T,
        requests[0],
        head_slots.reshape(segs, SEG),
        relation_slots.reshape(segs, SEG),
        tail_slots.reshape(segs, SEG),
        neg_offsets.T,
    )
    steps = d // 80
    at_loss = LANE // rest * rest - 2

    def rows(n):
        return pl.BlockSpec((d // steps, n), lambda i: (i, 0))

    outs = pl.pallas_call(
        functools.partial(adamw_kernel, at_loss + 1),
        grid=(steps,),
        out_shape=[jax.ShapeDtypeStruct((d, n), t) for n in (ne, nr) for t in (F32, F32, F32, BF16)],
        in_specs=[pl.BlockSpec((8, LANE), lambda i: (0, 0))] + [rows(ne)] * 4 + [rows(nr)] * 4,
        out_specs=[rows(ne)] * 4 + [rows(nr)] * 4,
        compiler_params=pltpu.CompilerParams(vmem_limit_bytes=32 * 1024 * 1024),
    )(
        stat,
        ge,
        entity_rows.T,
        entity_first.T,
        entity_second.T,
        gr,
        relation_rows.T,
        relation_first.T,
        relation_second.T,
    )
    e_new, e_one, e_two, e_low, r_new, r_one, r_two, r_low = (x.T for x in outs)
    return (
        e_new,
        e_one,
        e_two,
        r_new,
        r_one,
        r_two,
        e_low,
        r_low,
        stat[0, at_loss : at_loss + 1],
        stat[0, at_loss + 1 : at_loss + 2],
    )


def solution(mesh):
    rows = P("shard", None)
    both = ("grp", "shard")
    return jax.shard_map(
        functools.partial(per_device, mesh.shape["shard"], mesh.shape["grp"]),
        mesh=mesh,
        in_specs=(
            rows,
            rows,
            rows,
            rows,
            rows,
            rows,
            P(both, None, None),
            P(both),
            P(both),
            P(both),
            P(both, None),
            P(both),
        ),
        out_specs=(rows,) * 8 + (P(), P()),
        check_vma=False,
    )
```

time: 293 us -> 75.7 us (0.26)
  blocking collectives: 80.5 us -> 0 us
  other arithmetic: 71.7 us -> 0 us
  Pallas kernels: 0 us -> 64.3 us
  waiting for transfers between devices: 42.5 us -> 0 us
  local copies, waits for them, and re-layouts: 48.1 us -> 9.63 us
  starting transfers between devices: 17.9 us -> 0 us
  matrix products: 16.3 us -> 0 us
  between operations: 15.6 us -> 1.5 us
    psum x2 -> x0, blocking collectives: 80.5 us -> none  [totals(): return lax.psum((loss_part, pair_part), ('grp', 'shard'))]
    pallas_call x0 -> x2, Pallas kernels: none -> 64.3 us  [the longest x1 58.3 us: per_device(): pl.pallas_call(functools.partial(exchange_kernel, ns, ng, (d, ne, nr, cap...]
    reduce_sum x5 -> x0, other arithmetic: 28.3 us -> none  [the longest x1 17.4 us: per_device(): row_total = jnp.sum(pair_matrix, axis=2)]
    scatter-add x3 -> x0, other arithmetic: 26.4 us -> none  [the longest x1 21.6 us: per_device(): jnp.zeros((slot_total, D), jnp.float32).at[all_slots].add(edge_grads)]
    psum x1 -> x0, waiting for transfers between devices: 26 us -> none  [per_device(): entity_sum, relation_sum = lax.psum((entity_grad, relation_grad), 'grp')]
    all_to_all x3 -> x0, starting transfers between devices: 17.9 us -> none  [the longest x1 7.26 us: per_device(): lax.all_to_all(requests[0], 'shard', split_axis=0, concat_axis=0, tiled=T...]
    all_to_all x3 -> x0, waiting for transfers between devices: 16.4 us -> none  [the longest x1 15.6 us: per_device(): lax.all_to_all(slot_grads.reshape(served.shape), 'shard', split_axis=0, c...]
    dot_general x3 -> x0, matrix products: 16.3 us -> none  [the longest x1 6.64 us: per_device(): jnp.einsum('sab,sbd->sad', pair_matrix, target_seg, precision=HIGH)]
  transfers between devices with their start and end apart: 4 -> 0, of which waited for: 3 -> 0; matrix products, arithmetic and copies ran while one was open for 3% -> 0% of each run, Pallas kernels for 0% -> 0%
where the time goes in v1:
time: 75.7 us; the launch traced here: 75.4 us
  Pallas kernels  64.3 us (85%)
  local copies, waits for them, and re-layouts  9.63 us (13%)
  between operations  1.5 us (2%)
    pallas_call x1, Pallas kernels, per_device(): pl.pallas_call(functools.partial(exchange_kernel, ns, ng, (d, ne, nr, cap...  58.3 us
    unnamed x18, local copies, waits for them, and re-layouts  9.04 us
    pallas_call x1, Pallas kernels, per_device(): pl.pallas_call(functools.partial(adamw_kernel, at_loss + 1), grid=(steps,...  5.95 us

profile of v1, /device:TPU:0, one launch (start us, length us, event | category | flops | bytes accessed | tf_op | source)
XLA Modules:
  0.0 75.4 jit_solution(13247625524498157004)
XLA Ops:
  0.6 0.0 copy-start
  0.7 0.0 copy-start.1
  1.5 58.3 %shard_map.195 = (f32[400,1024]{1,0:T(8,128)}, f32[400,784]{1,0:T(8,128)}, f32[8,128]{1,0:T(8,128)}) custom-call(s32[1]{0:T(128)S(6)} %copy.22.valid_ref, f32[400,1024]{1,0:T(8,128)} %bitcast.21, f32[400,784]{1,0:T(8,128)} %bitcast.23, s32[8,40]{1,0:T(8,128)} %bitcast.30, s32[8,128]{1,0:T(8,128)} %bitcast.31, s32[8,128]{1,0:T(8,128)} %bitcast.32, ...), custom_call_target="tpu_custom_call" | custom-call | tf_op jit(solution)/shard_map/pallas_call | solution.py:594
  59.8 0.0 copy-done
  59.8 0.0 copy-done.1
  59.8 0.0 copy-start.2
  59.8 1.4 %copy-done.2 = f32[1024,400]{0,1:T(8,128)S(1)} copy-done((f32[1024,400]{0,1:T(8,128)S(1)}, f32[1024,400]{0,1:T(8,128)}, u32[]{:S(2)}) %copy-start.2) | copy-done | bytes 1638424
  61.2 0.0 copy-start.3
  61.2 1.4 %copy-done.3 = f32[1024,400]{0,1:T(8,128)S(1)} copy-done((f32[1024,400]{0,1:T(8,128)S(1)}, f32[1024,400]{0,1:T(8,128)}, u32[]{:S(2)}) %copy-start.3) | copy-done | bytes 1638424
  62.7 0.0 copy-start.4
  62.7 1.4 %copy-done.4 = f32[400,1024]{1,0:T(8,128)S(1)} copy-done((f32[400,1024]{1,0:T(8,128)S(1)}, f32[400,1024]{1,0:T(8,128)}, u32[]{:S(2)}) %copy-start.4) | copy-done | bytes 1638424
  64.1 0.0 copy-start.5
  64.1 1.4 %copy-done.5 = f32[784,400]{0,1:T(8,128)S(1)} copy-done((f32[784,400]{0,1:T(8,128)S(1)}, f32[784,400]{0,1:T(8,128)}, u32[]{:S(2)}) %copy-start.5) | copy-done | bytes 1254424
  65.5 0.0 copy-start.6
  65.5 1.4 %copy-done.6 = f32[784,400]{0,1:T(8,128)S(1)} copy-done((f32[784,400]{0,1:T(8,128)S(1)}, f32[784,400]{0,1:T(8,128)}, u32[]{:S(2)}) %copy-start.6) | copy-done | bytes 1254424
  66.8 0.0 copy-start.7
  66.8 1.4 %copy-done.7 = f32[400,784]{1,0:T(8,128)S(1)} copy-done((f32[400,784]{1,0:T(8,128)S(1)}, f32[400,784]{1,0:T(8,128)}, u32[]{:S(2)}) %copy-start.7) | copy-done | bytes 1254424
  68.2 0.0 copy-start.8
  68.2 0.7 copy-done.8
  68.9 5.9 %shard_map.196 = (f32[400,1024]{1,0:T(8,128)}, f32[400,1024]{1,0:T(8,128)}, f32[400,1024]{1,0:T(8,128)}, bf16[400,1024]{1,0:T(8,128)(2,1)}, f32[400,784]{1,0:T(8...) custom-call(f32[8,128]{1,0:T(8,128)S(1)} %copy-done.8, f32[400,1024]{1,0:T(8,128)S(1)} %copy-done.4, ...), custom_call_target="tpu_custom_call" | custom-call | tf_op jit(solution)/shard_map/pallas_call | solution.py:666
  74.8 0.6 fusion
Async XLA Ops:
  0.6 59.1 %copy-start = (f32[1024,400]{0,1:T(8,128)S(1)}, f32[1024,400]{0,1:T(8,128)}, u32[]{:S(2)}) copy-start(f32[1024,400]{0,1:T(8,128)} %param.12) | copy-start | bytes 4915204
  0.7 59.1 %copy-start.1 = (f32[784,400]{0,1:T(8,128)S(1)}, f32[784,400]{0,1:T(8,128)}, u32[]{:S(2)}) copy-start(f32[784,400]{0,1:T(8,128)} %param.15) | copy-start | bytes 3763204
  59.8 1.4 %copy-start.2 = (f32[1024,400]{0,1:T(8,128)S(1)}, f32[1024,400]{0,1:T(8,128)}, u32[]{:S(2)}) copy-start(f32[1024,400]{0,1:T(8,128)} %param.13) | copy-start | bytes 4915204
  61.2 1.4 %copy-start.3 = (f32[1024,400]{0,1:T(8,128)S(1)}, f32[1024,400]{0,1:T(8,128)}, u32[]{:S(2)}) copy-start(f32[1024,400]{0,1:T(8,128)} %param.14) | copy-start | bytes 4915204
  62.7 1.4 %copy-start.4 = (f32[400,1024]{1,0:T(8,128)S(1)}, f32[400,1024]{1,0:T(8,128)}, u32[]{:S(2)}) copy-start(f32[400,1024]{1,0:T(8,128)} %get-tuple-element.22.refs_0_) | copy-start | bytes 4915204
  64.1 1.4 %copy-start.5 = (f32[784,400]{0,1:T(8,128)S(1)}, f32[784,400]{0,1:T(8,128)}, u32[]{:S(2)}) copy-start(f32[784,400]{0,1:T(8,128)} %param.16) | copy-start | bytes 3763204
  65.5 1.4 %copy-start.6 = (f32[784,400]{0,1:T(8,128)S(1)}, f32[784,400]{0,1:T(8,128)}, u32[]{:S(2)}) copy-start(f32[784,400]{0,1:T(8,128)} %param.17) | copy-start | bytes 3763204
  66.8 1.4 %copy-start.7 = (f32[400,784]{1,0:T(8,128)S(1)}, f32[400,784]{1,0:T(8,128)}, u32[]{:S(2)}) copy-start(f32[400,784]{1,0:T(8,128)} %get-tuple-element.23.refs_4_) | copy-start | bytes 3763204
  68.2 0.7 copy-start.8

commit v2 on v1

--- a/solution.py
+++ b/solution.py
@@ -1,4 +1,5 @@
 import functools
+import math
 
 import jax
 import jax.numpy as jnp
@@ -46,8 +47,10 @@
     return lax.broadcasted_iota(I32, shape, axis)
 
 
-def far_first(n):
-    return sorted(range(1, n), key=lambda k: (abs(k - n // 2), k))
+def padded(ref):
+    *lead, rows, cols = ref.shape
+    size = jnp.dtype(ref.dtype).itemsize
+    return math.prod(lead) * up(rows, 32 // size) * up(cols, LANE) * size
 
 
 def exchange_kernel(
@@ -56,7 +59,11 @@
     dims,
     valid_ref,
     ent_hbm,
+    one_e_hbm,
+    two_e_hbm,
     rel_hbm,
+    one_r_hbm,
+    two_r_hbm,
     req_hbm,
     head_hbm,
     rslot_hbm,
@@ -66,7 +73,11 @@
     gr_ref,
     stat_ref,
     ent_v,
+    one_e_v,
+    two_e_v,
     rel_v,
+    one_r_v,
+    two_r_v,
     req_v,
     slots_v,
     neg_v,
@@ -123,13 +134,18 @@
     g = lax.axis_index("grp")
     s = lax.axis_index("shard")
     mate = g + 1 - 2 * lax.rem(g, 2)
-    order = far_first(ns)
+    near = list(range(1, ns))
+    order = near[ns // 2 - 1 :] + near[: ns // 2 - 1]
 
     def shard_at(k):
-        return lax.rem(s + k, ns)
-
-    def shard_from(k):
-        return lax.rem(s + ns - k, ns)
+        partner, bit = s, 1
+        while bit < ns:
+            if k & bit:
+                partner = partner + bit * (1 - 2 * lax.rem(s // bit, 2))
+            bit *= 2
+        return partner
+
+    shard_from = shard_at
 
     barrier = pltpu.get_barrier_semaphore()
     for k in range(1, ns):
@@ -148,6 +164,10 @@
                 (rslot_hbm, slots_v.at[1]),
                 (tail_hbm, slots_v.at[2]),
                 (neg_hbm, neg_v),
+                (one_e_hbm, one_e_v),
+                (two_e_hbm, two_e_v),
+                (one_r_hbm, one_r_v),
+                (two_r_hbm, two_r_v),
             ]
         )
     ]
@@ -296,7 +316,7 @@
     for k in range(1, ng):
         idg_copy(k).start()
 
-    for copy in local[3:]:
+    for copy in local[3:7]:
         copy.wait()
     slots = slots_v[...]
     owner = lax.shift_right_logical(slots * ((1 << 16) // cap + 1), 16)
@@ -432,7 +452,7 @@
         fetch_copy(k).wait_send()
     for r in range(ns):
         pack(r, True, extra)
-    for k in order:
+    for k in near:
         grad_copy(k).start()
     gbuf[g, s] = send_buf[s]
 
@@ -451,7 +471,7 @@
     def hand_over(dy, src):
         return block_copy(group_down(dy), src, mate, core_send.at[dy, src])
 
-    sequence = [0] + order
+    sequence = [0] + near
     lag = 2
 
     def hand_over_all(idx):
@@ -526,6 +546,8 @@
 
     stat_ref[...] = lax.fori_loop(0, ng, stat, jnp.zeros((8, LANE), F32))
 
+    for copy in local[7:]:
+        copy.wait()
     for k in order:
         ids_copy(k).wait_send()
         grad_copy(k).wait_send()
@@ -539,23 +561,80 @@
             hand_over(dy, src).wait_send()
 
 
-def adamw_kernel(at_pairs, stat_ref, *refs):
-    factor = 1.0 / stat_ref[0:1, at_pairs : at_pairs + 1]
-    fix_one = 1.0 - BETA_ONE**STEP
-    fix_two = 1.0 - BETA_TWO**STEP
-    for i in range(2):
-        g_ref, w_ref, one_ref, two_ref = refs[4 * i : 4 * i + 4]
-        w_out, one_out, two_out, low_out = refs[8 + 4 * i : 12 + 4 * i]
-        gradient = g_ref[...] * factor
-        weight = w_ref[...]
-        one = BETA_ONE * one_ref[...] + (1.0 - BETA_ONE) * gradient
-        two = BETA_TWO * two_ref[...] + (1.0 - BETA_TWO) * gradient * gradient
-        direction = one / fix_one / (jnp.sqrt(two / fix_two) + EPS_ADAM)
-        new = weight - RATE * (direction + DECAY * weight)
-        w_out[...] = new
-        one_out[...] = one
-        two_out[...] = two
-        low_out[...] = new.astype(BF16)
+def adamw_kernel(
+    at_loss,
+    strip,
+    stat_ref,
+    ge_ref,
+    gr_ref,
+    w_e,
+    one_e,
+    two_e,
+    w_r,
+    one_r,
+    two_r,
+    e_new,
+    e_one,
+    e_two,
+    e_low,
+    r_new,
+    r_one,
+    r_two,
+    r_low,
+    loss_ref,
+    pairs_ref,
+    *scratch,
+):
+    d = ge_ref.shape[0]
+    sems = scratch[-1]
+    total = stat_ref[0:1, :]
+    loss_ref[0] = total[0, at_loss]
+    pairs_ref[0] = total[0, at_loss + 1]
+    factor = ((1.0 - BETA_ONE) / total)[0, at_loss + 1]
+    square = (1.0 - BETA_TWO) / (1.0 - BETA_ONE) ** 2
+    fix_two = 1.0 / (1.0 - BETA_TWO**STEP)
+    rate = RATE / (1.0 - BETA_ONE**STEP)
+    tables = (
+        (ge_ref, w_e, one_e, two_e, (e_new, e_one, e_two, e_low), scratch[0:4]),
+        (gr_ref, w_r, one_r, two_r, (r_new, r_one, r_two, r_low), scratch[4:8]),
+    )
+
+    def copies(i):
+        at = pl.ds(pl.multiple_of(i * strip, strip), strip)
+        out = []
+        for n, (_, _, _, _, outs, bufs) in enumerate(tables):
+            for m, (hbm, buf) in enumerate(zip(outs, bufs)):
+                out.append(pltpu.make_async_copy(buf.at[at, :], hbm.at[at, :], sems.at[n * 4 + m, i]))
+        return out
+
+    def step(i, _):
+        for g_ref, w_ref, one_ref, two_ref, _, bufs in tables:
+
+            def rows(j, _):
+                at = pl.ds(pl.multiple_of(i * strip + j * 16, 16), 16)
+                gradient = g_ref[at, :] * factor
+                weight = w_ref[at, :]
+                one = BETA_ONE * one_ref[at, :] + gradient
+                two = BETA_TWO * two_ref[at, :] + square * gradient * gradient
+                scaled = two * fix_two
+                root = scaled * lax.rsqrt(scaled) + EPS_ADAM
+                new = weight * (1.0 - RATE * DECAY) - rate * one / root
+                bufs[0][at, :] = new
+                bufs[1][at, :] = one
+                bufs[2][at, :] = two
+                bufs[3][at, :] = new.astype(BF16)
+                return 0
+
+            lax.fori_loop(0, strip // 16, rows, 0, unroll=True)
+        for copy in copies(i):
+            copy.start()
+        return 0
+
+    steps = d // strip
+    lax.fori_loop(0, steps, step, 0)
+    for i in range(steps):
+        for copy in copies(i):
+            copy.wait()
 
 
 def per_device(
@@ -591,109 +670,94 @@
     vmem = pl.BlockSpec(memory_space=pltpu.VMEM)
     smem = pl.BlockSpec(memory_space=pltpu.SMEM)
     dma = pltpu.SemaphoreType.DMA
-    ge, gr, stat = pl.pallas_call(
+    hbm = functools.partial(pltpu.with_memory_space_constraint, memory_space=pltpu.HBM)
+    scratch = [
+        pltpu.VMEM((ns, cap), I32),
+        pltpu.VMEM((3, segs, SEG), I32),
+        pltpu.VMEM((neg, edges), I32),
+        pltpu.VMEM((dp, ne), BF16),
+        pltpu.VMEM((dp, ne), BF16),
+        pltpu.VMEM((dp, nrp), BF16),
+        pltpu.VMEM((dp, nrp), BF16),
+        pltpu.VMEM((ns, ns, cap), I32),
+        pltpu.VMEM((ng, ns, cap), I32),
+        pltpu.VMEM((ns, *block), F32),
+        pltpu.VMEM((ns, *block), F32),
+        pltpu.VMEM((ke, dp), F32),
+        pltpu.VMEM((kr, dp), F32),
+        pltpu.VMEM((ke, ne), BF16),
+        pltpu.VMEM((kr, nrp), BF16),
+        pltpu.VMEM((edges, ke), BF16),
+        pltpu.VMEM((edges, ke), BF16),
+        pltpu.VMEM((edges, 2 * kr), BF16),
+        pltpu.VMEM((ke, 2 * edges), BF16),
+        pltpu.VMEM((kr, edges), BF16),
+        pltpu.VMEM((segs, SEG, SEG), F32),
+        pltpu.VMEM((ke, dp), BF16),
+        pltpu.VMEM((ke, dp), BF16),
+        pltpu.VMEM((2 * kr, dp), BF16),
+        pltpu.VMEM((2 * edges, dp), BF16),
+        pltpu.VMEM((2 * edges, dp), BF16),
+        pltpu.VMEM((ng, ns, *block), F32),
+        pltpu.VMEM((d, 2 * ke), BF16),
+        pltpu.VMEM((d, 2 * kr), BF16),
+        dma((11,)),
+        dma((ns,)),
+        dma((ns,)),
+        dma((ng,)),
+        dma((ng,)),
+        dma((ns,)),
+        dma((ns,)),
+        dma((ns,)),
+        dma((ng, ns)),
+        dma((ny, ns)),
+        dma((max(ny - 1, 1), ns)),
+    ]
+    limit = sum(padded(x) for x in scratch[: scratch.index(dma((11,)))]) + (2 << 20)
+    passed = pl.pallas_call(
         functools.partial(exchange_kernel, ns, ng, (d, ne, nr, cap, edges, neg)),
         out_shape=(
-            jax.ShapeDtypeStruct((d, ne), F32),
-            jax.ShapeDtypeStruct((d, nr), F32),
-            jax.ShapeDtypeStruct((8, LANE), F32),
-        ),
-        in_specs=[smem] + [any_space] * 7,
-        out_specs=(vmem, vmem, vmem),
-        scratch_shapes=[
             pltpu.VMEM((d, ne), F32),
             pltpu.VMEM((d, nr), F32),
-            pltpu.VMEM((ns, cap), I32),
-            pltpu.VMEM((3, segs, SEG), I32),
-            pltpu.VMEM((neg, edges), I32),
-            pltpu.VMEM((dp, ne), BF16),
-            pltpu.VMEM((dp, ne), BF16),
-            pltpu.VMEM((dp, nrp), BF16),
-            pltpu.VMEM((dp, nrp), BF16),
-            pltpu.VMEM((ns, ns, cap), I32),
-            pltpu.VMEM((ng, ns, cap), I32),
-            pltpu.VMEM((ns, *block), F32),
-            pltpu.VMEM((ns, *block), F32),
-            pltpu.VMEM((ke, dp), F32),
-            pltpu.VMEM((kr, dp), F32),
-            pltpu.VMEM((ke, ne), BF16),
-            pltpu.VMEM((kr, nrp), BF16),
-            pltpu.VMEM((edges, ke), BF16),
-            pltpu.VMEM((edges, ke), BF16),
-            pltpu.VMEM((edges, 2 * kr), BF16),
-            pltpu.VMEM((ke, 2 * edges), BF16),
-            pltpu.VMEM((kr, edges), BF16),
-            pltpu.VMEM((segs, SEG, SEG), F32),
-            pltpu.VMEM((ke, dp), BF16),
-            pltpu.VMEM((ke, dp), BF16),
-            pltpu.VMEM((2 * kr, dp), BF16),
-            pltpu.VMEM((2 * edges, dp), BF16),
-            pltpu.VMEM((2 * edges, dp), BF16),
-            pltpu.VMEM((ng, ns, *block), F32),
-            pltpu.VMEM((d, 2 * ke), BF16),
-            pltpu.VMEM((d, 2 * kr), BF16),
-            dma((7,)),
-            dma((ns,)),
-            dma((ns,)),
-            dma((ng,)),
-            dma((ng,)),
-            dma((ns,)),
-            dma((ns,)),
-            dma((ns,)),
-            dma((ng, ns)),
-            dma((ny, ns)),
-            dma((max(ny - 1, 1), ns)),
-        ],
+            pltpu.VMEM((8, LANE), F32),
+        )
+        + (pltpu.VMEM((d, ne), F32),) * 3
+        + (pltpu.VMEM((d, nr), F32),) * 3,
+        in_specs=[smem] + [any_space] * 11,
+        out_specs=(vmem,) * 9,
+        scratch_shapes=scratch,
         compiler_params=pltpu.CompilerParams(
-            collective_id=0, has_side_effects=True, vmem_limit_bytes=60 * 1024 * 1024
+            collective_id=0, has_side_effects=True, vmem_limit_bytes=limit
         ),
     )(
         valid_counts,
-        entity_rows.T,
-        relation_rows.T,
-        requests[0],
-        head_slots.reshape(segs, SEG),
-        relation_slots.reshape(segs, SEG),
-        tail_slots.reshape(segs, SEG),
-        neg_offsets.T,
+        hbm(entity_rows.T),
+        hbm(entity_first.T),
+        hbm(entity_second.T),
+        hbm(relation_rows.T),
+        hbm(relation_first.T),
+        hbm(relation_second.T),
+        hbm(requests[0]),
+        hbm(head_slots.reshape(segs, SEG)),
+        hbm(relation_slots.reshape(segs, SEG)),
+        hbm(tail_slots.reshape(segs, SEG)),
+        hbm(neg_offsets.T),
     )
-    steps = d // 80
+    ge, gr, stat, *tables = passed
     at_loss = LANE // rest * rest - 2
-
-    def rows(n):
-        return pl.BlockSpec((d // steps, n), lambda i: (i, 0))
-
-    outs = pl.pallas_call(
-        functools.partial(adamw_kernel, at_loss + 1),
-        grid=(steps,),
-        out_shape=[jax.ShapeDtypeStruct((d, n), t) for n in (ne, nr) for t in (F32, F32, F32, BF16)],
-        in_specs=[pl.BlockSpec((8, LANE), lambda i: (0, 0))] + [rows(ne)] * 4 + [rows(nr)] * 4,
-        out_specs=[rows(ne)] * 4 + [rows(nr)] * 4,
+    strip = 80
+    shapes = [(jax.ShapeDtypeStruct((d, n), t)) for n in (ne, nr) for t in (F32, F32, F32, BF16)]
+    one = jax.ShapeDtypeStruct((1,), F32)
+    *outs, loss, pairs = pl.pallas_call(
+        functools.partial(adamw_kernel, at_loss, strip),
+        out_shape=shapes + [one, one],
+        in_specs=[vmem] * 9,
+        out_specs=[any_space] * 8 + [smem, smem],
+        scratch_shapes=[pltpu.VMEM(x.shape, x.dtype) for x in shapes] + [dma((8, d // strip))],
         compiler_params=pltpu.CompilerParams(vmem_limit_bytes=32 * 1024 * 1024),
-    )(
-        stat,
-        ge,
-        entity_rows.T,
-        entity_first.T,
-        entity_second.T,
-        gr,
-        relation_rows.T,
-        relation_first.T,
-        relation_second.T,
-    )
+    )(stat, ge, gr, *tables)
     e_new, e_one, e_two, e_low, r_new, r_one, r_two, r_low = (x.T for x in outs)
-    return (
-        e_new,
-        e_one,
-        e_two,
-        r_new,
-        r_one,
-        r_two,
-        e_low,
-        r_low,
-        stat[0, at_loss : at_loss + 1],
-        stat[0, at_loss + 1 : at_loss + 2],
-    )
+    return (e_new, e_one, e_two, r_new, r_one, r_two, e_low, r_low, loss, pairs)
 
 
 def solution(mesh):

time: 75.7 us -> 61.5 us (0.81)
  local copies, waits for them, and re-layouts: 9.63 us -> 0 us
  Pallas kernels: 64.3 us -> 60 us
    unnamed x18 -> x0, local copies, waits for them, and re-layouts: 9.04 us -> none
    pallas_call x1, Pallas kernels: 58.3 us -> 54.7 us  [per_device(): pl.pallas_call(functools.partial(exchange_kernel, ns, ng, (d, ne, nr, cap...]
where the time goes in v2:
time: 61.5 us; the launch traced here: 61.3 us
  Pallas kernels  60 us (98%)
  between operations  1.3 us (2%)
    pallas_call x1, Pallas kernels, per_device(): pl.pallas_call(functools.partial(exchange_kernel, ns, ng, (d, ne, nr, cap...  54.7 us
    pallas_call x1, Pallas kernels, per_device(): pl.pallas_call(functools.partial(adamw_kernel, at_loss, strip), out_shape...  5.32 us

profile of v2, /device:TPU:0, one launch (start us, length us, event | category | flops | bytes accessed | tf_op | source)
XLA Modules:
  0.0 61.3 jit_solution(3840915416410455679)
XLA Ops:
  1.3 54.7 %shard_map.195 = (f32[400,1024]{1,0:T(8,128)S(1)}, f32[400,784]{1,0:T(8,128)S(1)}, f32[8,128]{1,0:T(8,128)S(1)}, f32[400,1024]{1,0:T(8,128)S(1)}, f32[400,1024]{...) custom-call(s32[1]{0:T(128)S(6)} %copy.22.valid_ref, ...), custom_call_target="tpu_custom_call" | custom-call | tf_op jit(solution)/shard_map/pallas_call | solution.py:717
  56.0 5.3 %shard_map.196 = (f32[400,1024]{1,0:T(8,128)}, f32[400,1024]{1,0:T(8,128)}, f32[400,1024]{1,0:T(8,128)}, bf16[400,1024]{1,0:T(8,128)(2,1)}, f32[400,784]{1,0:T(8...) custom-call(f32[8,128]{1,0:T(8,128)S(1)} %get-tuple-element.29.stat_ref,, ...), custom_call_target="tpu_custom_call" | custom-call | tf_op jit(solution)/shard_map/pallas_call | solution.py:751

commit v3 on v2

--- a/solution.py
+++ b/solution.py
@@ -57,27 +57,34 @@
     ns,
     ng,
     dims,
+    keep,
     valid_ref,
-    ent_hbm,
-    one_e_hbm,
-    two_e_hbm,
-    rel_hbm,
-    one_r_hbm,
-    two_r_hbm,
     req_hbm,
     head_hbm,
     rslot_hbm,
     tail_hbm,
     neg_hbm,
+    ent_hbm,
+    rel_hbm,
+    *refs,
+):
+    rest_hbm, refs = refs[: 4 * keep], refs[4 * keep :]
+    ge_ref, gr_ref, stat_ref, ent_v, rel_v, *refs = refs
+    rest_v, refs = refs[: 4 * keep], refs[4 * keep :]
+    exchange(ns, ng, dims, valid_ref, (req_hbm, head_hbm, rslot_hbm, tail_hbm, neg_hbm), (ent_hbm, rel_hbm, *rest_hbm), ge_ref, gr_ref, stat_ref, (ent_v, rel_v, *rest_v), *refs)
+
+
+def exchange(
+    ns,
+    ng,
+    dims,
+    valid_ref,
+    small_hbm,
+    tables_hbm,
     ge_ref,
     gr_ref,
     stat_ref,
-    ent_v,
-    one_e_v,
-    two_e_v,
-    rel_v,
-    one_r_v,
-    two_r_v,
+    tables,
     req_v,
     slots_v,
     neg_v,
@@ -96,14 +103,20 @@
     hot_h,
     hot_t,
     hot_r,
+    hotx,
     hott,
-    hott_r,
     wt,
     eh,
     el,
     rr,
-    gg_h,
-    gg_l,
+    targets,
+    anchors,
+    folds,
+    squares,
+    edge_rows,
+    form,
+    y_h,
+    y_l,
     gbuf,
     sgt_e,
     sgt_r,
@@ -120,6 +133,9 @@
     y_send,
 ):
     d, ne, nr, cap, edges, neg = dims
+    ent_v, rel_v = tables[:2]
+    req_hbm, head_hbm, rslot_hbm, tail_hbm, neg_hbm = small_hbm
+    ent_hbm, rel_hbm = tables_hbm[:2]
     cap_r = cap - CAP_E
     ke, kr = ns * CAP_E, ns * cap_r
     chunks = d // LANE
@@ -164,10 +180,7 @@
                 (rslot_hbm, slots_v.at[1]),
                 (tail_hbm, slots_v.at[2]),
                 (neg_hbm, neg_v),
-                (one_e_hbm, one_e_v),
-                (two_e_hbm, two_e_v),
-                (one_r_hbm, one_r_v),
-                (two_r_hbm, two_r_v),
+                *zip(tables_hbm[2:], tables[2:]),
             ]
         )
     ]
@@ -327,11 +340,9 @@
     for i in range(segs):
         at = slice(i * SEG, (i + 1) * SEG)
         head_row, rel_row, tail_row = (v[i : i + 1, :] for v in (head_k, rel_k, tail_k))
-        hott[:, at] = jnp.where(iota((ke, SEG), 0) == head_row, 1.0, 0.0).astype(BF16)
-        hott[:, edges + i * SEG : edges + (i + 1) * SEG] = jnp.where(
-            iota((ke, SEG), 0) == tail_row, 1.0, 0.0
-        ).astype(BF16)
-        hott_r[:, at] = jnp.where(iota((kr, SEG), 0) == rel_row, 1.0, 0.0).astype(BF16)
+        hotx[0:ke, at] = jnp.where(iota((ke, SEG), 0) == head_row, 1.0, 0.0).astype(BF16)
+        hott[:, at] = jnp.where(iota((ke, SEG), 0) == tail_row, 1.0, 0.0).astype(BF16)
+        hotx[ke:, at] = jnp.where(iota((kr, SEG), 0) == rel_row, 1.0, 0.0).astype(BF16)
         head_col, rel_col, tail_col = (
             jnp.broadcast_to(v.astype(F32), (SEG, SEG)).T[:, 0:1] for v in (head_row, rel_row, tail_row)
         )
@@ -383,23 +394,38 @@
             out += x[:, c * LANE : (c + 1) * LANE]
         return out
 
-    def edge_step(i, loss):
-        at = pl.ds(pl.multiple_of(i * SEG, SEG), SEG)
-        at_t = pl.ds(pl.multiple_of(edges + i * SEG, SEG), SEG)
-        a = mm(hot_h[at, :], eh[...]) + mm(hot_h[at, :], el[...]) + mm(hot_r[at, :], rr[...])
-        t = mm(hot_t[at, :], eh[...]) + mm(hot_t[at, :], el[...])
-        ah, al = halves(a)
-        th, tl = halves(t)
-        aa = jnp.concatenate([ah, al], axis=0)
-        tt = jnp.concatenate([th, tl], axis=0)
+    def seg(i):
+        return slice(i * SEG, (i + 1) * SEG)
+
+    def pair(i):
+        return slice(2 * i * SEG, 2 * (i + 1) * SEG)
+
+    for i in range(segs):
+        hots = jnp.concatenate([hot_h[seg(i), :], hot_t[seg(i), :]], axis=0)
+        both_h = mm(hots, eh[...])
+        both_l = mm(hots, el[...])
+        a = both_h[0:SEG] + both_l[0:SEG] + mm(hot_r[seg(i), :], rr[...])
+        t = both_h[SEG:] + both_l[SEG:]
+        targets[pair(i), :] = jnp.concatenate([both_h[SEG:].astype(BF16), both_l[SEG:].astype(BF16)], axis=0)
+        anchors[pair(i), :] = jnp.concatenate(halves(a), axis=0)
         offset = a - t
-        dist_pos = jnp.sqrt(jnp.sum(lane_fold(offset * offset).T, axis=0, keepdims=True) + EPS_DIST)
-        anchor_sq = jnp.sum(lane_fold(a * a).T, axis=0, keepdims=True)
-        target_sq = jnp.sum(lane_fold(t * t), axis=1, keepdims=True)
-        near = mm_nt(th, aa)
-        far = mm_nt(tl, aa)
-        gram = near[:, 0:SEG] + (near[:, SEG:] + far[:, 0:SEG] + far[:, SEG:])
-        square = jnp.maximum(anchor_sq + target_sq - 2.0 * gram, 0.0) + EPS_DIST
+        folds[0, i] = lane_fold(offset * offset)
+        folds[1, i] = lane_fold(a * a)
+        folds[2, i] = lane_fold(t * t)
+
+    for i in range(segs):
+        terms = mm_nt(targets[pair(i), :], anchors[pair(i), :])
+        gram = terms[0:SEG, 0:SEG] + (terms[0:SEG, SEG:] + terms[SEG:, 0:SEG] + terms[SEG:, SEG:])
+        square_pos = jnp.sum(folds[0, i].T, axis=0, keepdims=True)
+        edge_rows[0:1, seg(i)] = jnp.sqrt(square_pos + EPS_DIST)
+        anchor_sq = jnp.sum(folds[1, i].T, axis=0, keepdims=True)
+        target_sq = jnp.sum(folds[2, i], axis=1, keepdims=True)
+        squares[i] = anchor_sq + target_sq - 2.0 * gram
+
+    loss = jnp.zeros((SEG, SEG), F32)
+    for i in range(segs):
+        square = jnp.maximum(squares[i], 0.0) + EPS_DIST
+        dist_pos = edge_rows[0:1, seg(i)]
         inv = lax.rsqrt(square)
         m = MARGIN + dist_pos - square * inv
         w = wt[i]
@@ -409,20 +435,46 @@
         ratio = jnp.sum(slope, axis=0, keepdims=True) / dist_pos
         pt = slope * inv - jnp.where(sub == lane, ratio, 0.0)
         pa = pt.T
-        row_t = jnp.sum(pt, axis=1, keepdims=True)
-        row_a = jnp.sum(pa, axis=1, keepdims=True)
-        pth, ptl = halves(pt)
-        pah, pal = halves(pa)
-        grad_t = mm(jnp.concatenate([pth, pth], axis=1), aa) + mm(ptl, ah) - row_t * t
-        grad_a = mm(jnp.concatenate([pah, pah], axis=1), tt) + mm(pal, th) - row_a * a
-        gg_h[at, :], gg_l[at, :] = halves(grad_a)
-        gg_h[at_t, :], gg_l[at_t, :] = halves(grad_t)
-        return loss
-
-    loss = jnp.sum(lax.fori_loop(0, segs, edge_step, jnp.zeros((SEG, SEG), F32)))
-
-    rows_e[...] = mm(hott[...], gg_h[...]) + mm(hott[...], gg_l[...])
-    rows_r[...] = mm(hott_r[...], gg_h[0:edges, :]) + mm(hott_r[...], gg_l[0:edges, :])
+        sum_a = jnp.sum(pt, axis=0, keepdims=True)
+        edge_rows[1:2, seg(i)] = sum_a
+        edge_rows[2:3, seg(i)] = jnp.sum(pa, axis=0, keepdims=True)
+        own_h, own_l = halves(jnp.where(sub == lane, -sum_a, 0.0))
+        pa_h, pa_l = halves(pa)
+        form[pair(i), 0:SEG] = jnp.concatenate([pa_h, pa_l], axis=0)
+        form[pair(i), SEG:] = jnp.concatenate([own_h, own_l], axis=0)
+    loss = jnp.sum(loss)
+
+    for i in range(segs):
+        hots = jnp.concatenate([hot_t[seg(i), :], hot_h[seg(i), :]], axis=0)
+        y = mm(form[pair(i), :], hots)
+        y_h[seg(i), :], y_l[seg(i), :] = halves(y[0:SEG] + y[SEG:])
+    crossed = mm(hotx[...], y_h[...]) + mm(hotx[...], y_l[...])
+    form_re = crossed[ke:]
+    own_e = jnp.zeros((ke, LANE), F32)
+    own_r = jnp.zeros((kr, LANE), F32)
+    for i in range(segs):
+        sum_a = edge_rows[1:2, seg(i)]
+        sum_t = edge_rows[2:3, seg(i)]
+        own_e += hotx[0:ke, seg(i)].astype(F32) * sum_a - hott[:, seg(i)].astype(F32) * sum_t
+        own_r -= hotx[ke:, seg(i)].astype(F32) * sum_a
+    own_e = jnp.sum(own_e, axis=1, keepdims=True)
+    own_r = jnp.sum(own_r, axis=1, keepdims=True)
+    diagonal = iota((ke, ke), 0) == iota((ke, ke), 1)
+    form_ee = crossed[0:ke] + crossed[0:ke].T + jnp.where(diagonal, own_e, 0.0)
+
+    ee_h, ee_l = halves(form_ee)
+    re_h, re_l = halves(form_re)
+    er_h, er_l = halves(form_re.T)
+    rows_e[...] = (
+        mm(ee_h, eh[...])
+        + (mm(ee_h, el[...]) + mm(ee_l, eh[...]))
+        + (mm(jnp.concatenate([er_h, er_h], axis=1), rr[...]) + mm(er_l, rr[0:kr, :]))
+    )
+    rows_r[...] = (
+        mm(re_h, eh[...])
+        + (mm(re_h, el[...]) + mm(re_l, eh[...]))
+        + own_r * (rr[0:kr, :].astype(F32) + rr[kr : 2 * kr, :].astype(F32))
+    )
     at_loss = copies * rest - 2
     extra = jnp.where(lane8 == at_loss, loss, jnp.where(lane8 == at_loss + 1, pairs, 0.0))
 
@@ -690,14 +742,20 @@
         pltpu.VMEM((edges, ke), BF16),
         pltpu.VMEM((edges, ke), BF16),
         pltpu.VMEM((edges, 2 * kr), BF16),
-        pltpu.VMEM((ke, 2 * edges), BF16),
-        pltpu.VMEM((kr, edges), BF16),
+        pltpu.VMEM((ke + kr, edges), BF16),
+        pltpu.VMEM((ke, edges), BF16),
         pltpu.VMEM((segs, SEG, SEG), F32),
         pltpu.VMEM((ke, dp), BF16),
         pltpu.VMEM((ke, dp), BF16),
         pltpu.VMEM((2 * kr, dp), BF16),
         pltpu.VMEM((2 * edges, dp), BF16),
         pltpu.VMEM((2 * edges, dp), BF16),
+        pltpu.VMEM((3, segs, SEG, SEG), F32),
+        pltpu.VMEM((segs, SEG, SEG), F32),
+        pltpu.VMEM((8, edges), F32),
+        pltpu.VMEM((2 * edges, 2 * SEG), BF16),
+        pltpu.VMEM((edges, ke), BF16),
+        pltpu.VMEM((edges, ke), BF16),
         pltpu.VMEM((ng, ns, *block), F32),
         pltpu.VMEM((d, 2 * ke), BF16),
         pltpu.VMEM((d, 2 * kr), BF16),
@@ -713,37 +771,40 @@
         dma((ny, ns)),
         dma((max(ny - 1, 1), ns)),
     ]
-    limit = sum(padded(x) for x in scratch[: scratch.index(dma((11,)))]) + (2 << 20)
-    passed = pl.pallas_call(
-        functools.partial(exchange_kernel, ns, ng, (d, ne, nr, cap, edges, neg)),
-        out_shape=(
-            pltpu.VMEM((d, ne), F32),
-            pltpu.VMEM((d, nr), F32),
-            pltpu.VMEM((8, LANE), F32),
-        )
-        + (pltpu.VMEM((d, ne), F32),) * 3
-        + (pltpu.VMEM((d, nr), F32),) * 3,
-        in_specs=[smem] + [any_space] * 11,
-        out_specs=(vmem,) * 9,
-        scratch_shapes=scratch,
+    small = [
+        requests[0],
+        head_slots.reshape(segs, SEG),
+        relation_slots.reshape(segs, SEG),
+        tail_slots.reshape(segs, SEG),
+        neg_offsets.T,
+    ]
+    rows = [entity_rows.T, relation_rows.T]
+    moments = [entity_first.T, entity_second.T, relation_first.T, relation_second.T]
+    sums = [pltpu.VMEM((d, ne), F32), pltpu.VMEM((d, nr), F32), pltpu.VMEM((8, LANE), F32)]
+    held_rows = [pltpu.VMEM(x.shape, F32) for x in rows]
+    held_moments = [pltpu.VMEM(x.shape, F32) for x in moments]
+    need = sum(padded(x) for x in scratch[: scratch.index(dma((11,)))]) + (2 << 20)
+    keep = need + sum(padded(x) for x in sums + held_rows + held_moments) < (62 << 20)
+    if keep:
+        outs, held = sums + held_rows + held_moments, []
+    else:
+        outs, held = sums, held_rows
+        need += sum(padded(x) for x in held)
+    operands = small + rows + (moments if keep else [])
+    ge, gr, stat, *passed = pl.pallas_call(
+        functools.partial(exchange_kernel, ns, ng, (d, ne, nr, cap, edges, neg), int(keep)),
+        out_shape=outs,
+        in_specs=[smem] + [any_space] * len(operands),
+        out_specs=[vmem] * len(outs),
+        scratch_shapes=held + scratch,
         compiler_params=pltpu.CompilerParams(
-            collective_id=0, has_side_effects=True, vmem_limit_bytes=limit
+            collective_id=0, has_side_effects=True, vmem_limit_bytes=need
         ),
-    )(
-        valid_counts,
-        hbm(entity_rows.T),
-        hbm(entity_first.T),
-        hbm(entity_second.T),
-        hbm(relation_rows.T),
-        hbm(relation_first.T),
-        hbm(relation_second.T),
-        hbm(requests[0]),
-        hbm(head_slots.reshape(segs, SEG)),
-        hbm(relation_slots.reshape(segs, SEG)),
-        hbm(tail_slots.reshape(segs, SEG)),
-        hbm(neg_offsets.T),
-    )
-    ge, gr, stat, *tables = passed
+    )(valid_counts, *[hbm(x) for x in operands])
+    if not keep:
+        passed = rows + moments
+    w_e, w_r, one_e, two_e, one_r, two_r = passed
+    tables = (w_e, one_e, two_e, w_r, one_r, two_r)
     at_loss = LANE // rest * rest - 2
     strip = 80
     shapes = [(jax.ShapeDtypeStruct((d, n), t)) for n in (ne, nr) for t in (F32, F32, F32, BF16)]

time: 61.5 us -> 57.1 us (0.928)
  Pallas kernels: 60 us -> 55.6 us
    pallas_call x1, Pallas kernels: 54.7 us -> 50.3 us  [per_device(): pl.pallas_call(functools.partial(exchange_kernel, ns, ng, (d, ne, nr, cap...]
where the time goes in v3:
time: 57.1 us; the launch traced here: 56.9 us
  Pallas kernels  55.6 us (97%)
  between operations  1.3 us (2%)
    pallas_call x1, Pallas kernels, per_device(): pl.pallas_call(functools.partial(exchange_kernel, ns, ng, (d, ne, nr, cap...  50.3 us
    pallas_call x1, Pallas kernels, per_device(): pl.pallas_call(functools.partial(adamw_kernel, at_loss, strip), out_shape...  5.31 us

profile of v3, /device:TPU:0, one launch (start us, length us, event | category | flops | bytes accessed | tf_op | source)
XLA Modules:
  0.0 56.9 jit_solution(4965040018606858449)
XLA Ops:
  1.3 50.3 %shard_map.195 = (f32[400,1024]{1,0:T(8,128)S(1)}, f32[400,784]{1,0:T(8,128)S(1)}, f32[8,128]{1,0:T(8,128)S(1)}, f32[400,1024]{1,0:T(8,128)S(1)}, f32[400,784]{1...) custom-call(s32[1]{0:T(128)S(6)} %copy.22.valid_ref, ...), custom_call_target="tpu_custom_call" | custom-call | tf_op jit(solution)/shard_map/pallas_call | solution.py:794
  51.6 5.3 %shard_map.196 = (f32[400,1024]{1,0:T(8,128)}, f32[400,1024]{1,0:T(8,128)}, f32[400,1024]{1,0:T(8,128)}, bf16[400,1024]{1,0:T(8,128)(2,1)}, f32[400,784]{1,0:T(8...) custom-call(f32[8,128]{1,0:T(8,128)S(1)} %get-tuple-element.29.stat_ref,, ...), custom_call_target="tpu_custom_call" | custom-call | tf_op jit(solution)/shard_map/pallas_call | solution.py:812

commit v4 on v3

--- a/solution.py
+++ b/solution.py
@@ -58,6 +58,7 @@
     ng,
     dims,
     keep,
+    early,
     valid_ref,
     req_hbm,
     head_hbm,
@@ -71,13 +72,14 @@
     rest_hbm, refs = refs[: 4 * keep], refs[4 * keep :]
     ge_ref, gr_ref, stat_ref, ent_v, rel_v, *refs = refs
     rest_v, refs = refs[: 4 * keep], refs[4 * keep :]
-    exchange(ns, ng, dims, valid_ref, (req_hbm, head_hbm, rslot_hbm, tail_hbm, neg_hbm), (ent_hbm, rel_hbm, *rest_hbm), ge_ref, gr_ref, stat_ref, (ent_v, rel_v, *rest_v), *refs)
+    exchange(ns, ng, dims, early, valid_ref, (req_hbm, head_hbm, rslot_hbm, tail_hbm, neg_hbm), (ent_hbm, rel_hbm, *rest_hbm), ge_ref, gr_ref, stat_ref, (ent_v, rel_v, *rest_v), *refs)
 
 
 def exchange(
     ns,
     ng,
     dims,
+    early,
     valid_ref,
     small_hbm,
     tables_hbm,
@@ -131,6 +133,7 @@
     g_recv,
     core_send,
     y_send,
+    turn_sem,
 ):
     d, ne, nr, cap, edges, neg = dims
     ent_v, rel_v = tables[:2]
@@ -149,9 +152,10 @@
 
     g = lax.axis_index("grp")
     s = lax.axis_index("shard")
-    mate = g + 1 - 2 * lax.rem(g, 2)
+    parity = lax.rem(g, 2)
+    mate = g + 1 - 2 * parity
     near = list(range(1, ns))
-    order = near[ns // 2 - 1 :] + near[: ns // 2 - 1]
+    order = near
 
     def shard_at(k):
         partner, bit = s, 1
@@ -184,7 +188,7 @@
             ]
         )
     ]
-    for copy in local:
+    for copy in local[:7]:
         copy.start()
     local[0].wait()
     pl.semaphore_wait(barrier, ns - 1 + ng - 1)
@@ -214,20 +218,13 @@
     local[1].wait()
     local[2].wait()
 
-    def split_rows(i, _):
-        at = pl.ds(pl.multiple_of(i * 16, 16), 16)
-        hi, lo = halves(ent_v[at, :])
-        eth[at, :] = hi
-        etl[at, :] = lo
-        hi, lo = halves(rel_v[at, :])
-        rth[at, 0:nr] = hi
-        rtl[at, 0:nr] = lo
-        return 0
-
+    for start in range(0, d, 80):
+        at = slice(start, start + 80)
+        eth[at, :], etl[at, :] = halves(ent_v[at, :])
+        rth[at, 0:nr], rtl[at, 0:nr] = halves(rel_v[at, :])
     if nrp > nr:
         rth[:, nr:nrp] = jnp.zeros((dp, nrp - nr), BF16)
         rtl[:, nr:nrp] = jnp.zeros((dp, nrp - nr), BF16)
-    lax.fori_loop(0, d // 16, split_rows, 0)
     for table in (eth, etl, rth, rtl):
         tail_rows = table[chunks * LANE : d, :]
         for c in range(1, copies):
@@ -257,23 +254,27 @@
             device_id={"grp": other},
         )
 
-    def one_hots(grp):
+    lanes_e = iota((CAP_E, ne), 1).astype(F32)
+    lanes_r = iota((cap_r, nrp), 1).astype(F32) + float(ne)
+
+    def one_hots(at, blocks, columns):
+        pieces = []
+        for n, (grp, src) in enumerate(blocks):
+            column = columns[grp][:, src : src + 1]
+            hit = jnp.where(column[0:CAP_E] == lanes_e, 1.0, 0.0).astype(BF16)
+            oh_e[at, n * CAP_E : (n + 1) * CAP_E, :] = hit
+            pieces.append(jnp.where(column[CAP_E:cap] == lanes_r, 1.0, 0.0))
+        hit = jnp.concatenate(pieces, axis=0).astype(BF16)
+        oh_r[at, 0:kr, :] = hit
+        oh_r[at, kr : 2 * kr, :] = hit
+
+    def columns_of(grp):
         wide = jnp.concatenate([idg[grp].astype(F32), jnp.zeros((ns, LANE - cap), F32)], axis=1)
-        columns = jnp.concatenate([wide] + [jnp.zeros((LANE - ns, LANE), F32)], axis=0).T
-        lanes_e = iota((CAP_E, ne), 1).astype(F32)
-        lanes_r = iota((cap_r, nrp), 1).astype(F32) + float(ne)
-        pieces = []
-        for r in range(ns):
-            column = columns[:, r : r + 1]
-            hit = jnp.where(column[0:CAP_E] == lanes_e, 1.0, 0.0).astype(BF16)
-            oh_e[r * CAP_E : (r + 1) * CAP_E, :] = hit
-            pieces.append(jnp.where(column[CAP_E:cap] == lanes_r, 1.0, 0.0))
-        for r in range(0, ns, 2):
-            oh_r[r * cap_r : (r + 2) * cap_r, :] = jnp.concatenate(pieces[r : r + 2], axis=0).astype(BF16)
-
-    one_hots(g)
-    rows_e[...] = mm_nt(oh_e[...], eth[...]) + mm_nt(oh_e[...], etl[...])
-    rows_r[...] = mm_nt(oh_r[...], rth[...]) + mm_nt(oh_r[...], rtl[...])
+        return jnp.concatenate([wide, jnp.zeros((LANE - ns, LANE), F32)], axis=0).T
+
+    one_hots(0, [(0, src) for src in range(ns)], [columns_of(g)])
+    rows_e[...] = mm_nt(oh_e[0], eth[...]) + mm_nt(oh_e[0], etl[...])
+    rows_r[...] = mm_nt(oh_r[0, 0:kr], rth[...]) + mm_nt(oh_r[0, 0:kr], rtl[...])
 
     lane8 = iota((8, LANE), 1)
 
@@ -323,11 +324,16 @@
 
     for r in range(ns):
         pack(r, False, jnp.zeros((8, LANE), F32))
-    for k in order:
-        fetch_copy(k).start()
+    @pl.when(parity == 0)
+    def _():
+        for k in order:
+            fetch_copy(k).start()
+
     recv_buf[s] = send_buf[s]
     for k in range(1, ng):
         idg_copy(k).start()
+    for copy in local[7:]:
+        copy.start()
 
     for copy in local[3:7]:
         copy.wait()
@@ -346,12 +352,35 @@
         head_col, rel_col, tail_col = (
             jnp.broadcast_to(v.astype(F32), (SEG, SEG)).T[:, 0:1] for v in (head_row, rel_row, tail_row)
         )
-        lanes_e = iota((SEG, ke), 1).astype(F32)
-        lanes_r = iota((SEG, kr), 1).astype(F32)
-        hot_h[at, :] = jnp.where(lanes_e == head_col, 1.0, 0.0).astype(BF16)
-        hot_t[at, :] = jnp.where(lanes_e == tail_col, 1.0, 0.0).astype(BF16)
-        hit = jnp.where(lanes_r == rel_col, 1.0, 0.0)
+        slots_e = iota((SEG, ke), 1).astype(F32)
+        slots_r = iota((SEG, kr), 1).astype(F32)
+        hot_h[at, :] = jnp.where(slots_e == head_col, 1.0, 0.0).astype(BF16)
+        hot_t[at, :] = jnp.where(slots_e == tail_col, 1.0, 0.0).astype(BF16)
+        hit = jnp.where(slots_r == rel_col, 1.0, 0.0)
         hot_r[at, :] = jnp.concatenate([hit, hit], axis=1).astype(BF16)
+
+    part = ns // 2
+    batches = [
+        ((core + 4 * pair_of, core + 4 * pair_of + 2), core, b * part)
+        for core in range(2)
+        for b in range(2)
+        for pair_of in range(ny // 2)
+    ]
+
+    def batch_one_hots(n):
+        groups, _, start = batches[n]
+        columns = []
+        for grp in groups:
+            wide = jnp.concatenate([idg[grp, pl.ds(shard_at(k), 1), :].astype(F32) for k in range(start, start + part)], axis=0)
+            wide = jnp.concatenate([wide, jnp.zeros((part, LANE - cap), F32)], axis=1)
+            columns.append(jnp.concatenate([wide, jnp.zeros((LANE - part, LANE), F32)], axis=0).T)
+        one_hots(n if early else 0, [(c, k) for c in range(2) for k in range(part)], columns)
+
+    for k in range(1, ng):
+        idg_arrival(k).wait_recv()
+    if early:
+        for n in range(len(batches)):
+            batch_one_hots(n)
 
     valid = valid_ref[0]
     sub = iota((SEG, SEG), 0)
@@ -369,10 +398,24 @@
 
     pairs = jnp.sum(lax.fori_loop(0, segs, count, jnp.zeros((SEG, SEG), F32)))
 
-    recv = [(s, None)] + [(shard_from(k), k) for k in order]
-    for src, k in recv:
-        if k is not None:
+    most = 4
+
+    @pl.when(parity == 0)
+    def _():
+        for k in order[:most]:
             fetch_arrival(k).wait_recv()
+        pl.semaphore_signal(turn_sem, inc=1, device_id={"grp": mate})
+        for k in order[most:]:
+            fetch_arrival(k).wait_recv()
+
+    @pl.when(parity == 1)
+    def _():
+        pl.semaphore_wait(turn_sem, 1)
+        for k in order:
+            fetch_copy(k).start()
+        for k in order:
+            fetch_arrival(k).wait_recv()
+
     for p in range(ns):
         ends_e, ends_r = last_columns(recv_buf[p, chunks * cap : chunks * cap + 8, :])
         e = jnp.concatenate(
@@ -515,81 +558,101 @@
         return lax.rem(g + ng - 2 * dy, ng)
 
     def forward(src):
-        out = [block_copy(g, src, mate, core_send.at[0, src])]
-        for dy in range(1, ny):
-            out.append(block_copy(g, src, group_up(dy), y_send.at[dy - 1, src]))
-        return out
+        out = [block_copy(g, src, group_up(dy), y_send.at[dy - 1, src]) for dy in range(1, ny)]
+        return out + [block_copy(g, src, mate, core_send.at[0, src])]
 
     def hand_over(dy, src):
         return block_copy(group_down(dy), src, mate, core_send.at[dy, src])
 
     sequence = [0] + near
     lag = 2
-
-    def hand_over_all(idx):
-        src = shard_from(sequence[idx])
+    handed = [0]
+
+    def hand_over_to(end):
+        end = max(end, handed[0])
+        for k in sequence[handed[0] : end]:
+            for dy in range(1, ny):
+                arrived(group_down(dy), shard_at(k))
+                hand_over(dy, shard_at(k)).start()
+        handed[0] = end
+
+    def hand_over_last():
         for dy in range(1, ny):
-            arrived(group_down(dy), src)
-            hand_over(dy, src).start()
-
-    for idx, k in enumerate(sequence):
-        src = shard_from(k)
-        if k:
-            arrived(g, src)
-        for copy in forward(src):
-            copy.start()
-        if idx >= lag:
-            hand_over_all(idx - lag)
-
-    def gather_blocks(grp):
-        for r in range(ns):
-            ends_e, ends_r = last_columns(gbuf[grp, r, chunks * cap : chunks * cap + 8, :])
-            rows_e[r * CAP_E : (r + 1) * CAP_E, chunks * LANE : dp] = ends_e
-            rows_r[r * cap_r : (r + 1) * cap_r, chunks * LANE : dp] = ends_r
-            for c in range(chunks):
-                at = slice(c * LANE, (c + 1) * LANE)
-                rows_e[r * CAP_E : (r + 1) * CAP_E, at] = gbuf[grp, r, c * cap : c * cap + CAP_E, :]
-                rows_r[r * cap_r : (r + 1) * cap_r, at] = gbuf[grp, r, c * cap + CAP_E : (c + 1) * cap, :]
+            arrived(group_down(dy), shard_at(sequence[-1]))
+            hand_over(dy, shard_at(sequence[-1])).start()
+
+    def add_batch(n):
+        groups, core, start = batches[n]
+
+        @pl.when(parity != core)
+        def _():
+            for k in range(start, start + part):
+                for grp in groups:
+                    arrived(grp, shard_at(k))
+
+        if not early:
+            batch_one_hots(n)
+        at = n if early else 0
+        blocks = [(grp, shard_at(k)) for grp in groups for k in range(start, start + part)]
+        ends = [last_columns(gbuf[grp, src, chunks * cap : chunks * cap + 8, :]) for grp, src in blocks]
         for c in range(chunks + 1):
-            at = slice(c * LANE, (c + 1) * LANE)
             size = LANE if c < chunks else rest
             put = slice(c * LANE, c * LANE + size)
-            hi, lo = halves(rows_e[:, at].T[0:size, :])
+            if c < chunks:
+                e = [gbuf[grp, src, c * cap : c * cap + CAP_E, :] for grp, src in blocks]
+                r = [gbuf[grp, src, c * cap + CAP_E : (c + 1) * cap, :] for grp, src in blocks]
+            else:
+                e, r = [x[0] for x in ends], [x[1] for x in ends]
+            hi, lo = halves(jnp.concatenate(e, axis=0).T[0:size, :])
             sgt_e[put, 0:ke] = hi
             sgt_e[put, ke : 2 * ke] = lo
-            hi, lo = halves(rows_r[:, at].T[0:size, :])
+            hi, lo = halves(jnp.concatenate(r, axis=0).T[0:size, :])
             sgt_r[put, 0:kr] = hi
             sgt_r[put, kr : 2 * kr] = lo
-
-    def add_group(grp, first):
-        gather_blocks(grp)
-        part_e = mm(sgt_e[:, 0:ke], oh_e[...]) + mm(sgt_e[:, ke : 2 * ke], oh_e[...])
-        part_r = mm(sgt_r[:, 0:kr], oh_r[...]) + mm(sgt_r[:, kr : 2 * kr], oh_r[...])
-        if first:
+        part_e = mm(sgt_e[:, 0:ke], oh_e[at]) + mm(sgt_e[:, ke : 2 * ke], oh_e[at])
+        part_r = mm(sgt_r[...], oh_r[at])
+        if n:
+            ge_ref[...] += part_e
+            gr_ref[...] += part_r[:, 0:nr]
+        else:
             ge_ref[...] = part_e
             gr_ref[...] = part_r[:, 0:nr]
-        else:
-            ge_ref[...] += part_e
-            gr_ref[...] += part_r[:, 0:nr]
-
-    one_hots(g)
-    add_group(g, True)
-    for idx in range(max(len(sequence) - lag, 0), len(sequence)):
-        hand_over_all(idx)
+
+    def pass_on(idx):
+        k = sequence[idx]
+        if k:
+            arrived(g, shard_at(k))
+        for copy in forward(shard_at(k)):
+            copy.start()
+
+    for idx in range(ns):
+        pass_on(idx)
+        hand_over_to(idx + 1 - lag)
+    for copy in local[7:]:
+        copy.wait()
+    for k in near:
+        ids_copy(k).wait_send()
+        grad_copy(k).wait_send()
     for k in range(1, ng):
-        idg_arrival(k).wait_recv()
-    one_hots(mate)
-    for k in sequence:
-        arrived(mate, shard_from(k))
-    add_group(mate, False)
-    for dy in range(1, ny):
-        one_hots(group_down(dy))
-        add_group(group_down(dy), False)
-        other = lax.rem(mate + ng - 2 * dy, ng)
-        one_hots(other)
-        for k in sequence:
-            arrived(other, shard_from(k))
-        add_group(other, False)
+        idg_copy(k).wait_send()
+    quarter = len(batches) // 4
+    for n in range(quarter):
+        add_batch(n)
+    hand_over_to(ns - 1)
+
+    @pl.when(parity == 0)
+    def _():
+        hand_over_last()
+
+    for n in range(quarter, 2 * quarter):
+        add_batch(n)
+
+    @pl.when(parity == 1)
+    def _():
+        hand_over_last()
+
+    for n in range(2 * quarter, 4 * quarter):
+        add_batch(n)
 
     def stat(i, total):
         for r in range(ns):
@@ -598,13 +661,6 @@
 
     stat_ref[...] = lax.fori_loop(0, ng, stat, jnp.zeros((8, LANE), F32))
 
-    for copy in local[7:]:
-        copy.wait()
-    for k in order:
-        ids_copy(k).wait_send()
-        grad_copy(k).wait_send()
-    for k in range(1, ng):
-        idg_copy(k).wait_send()
     for k in sequence:
         src = shard_from(k)
         for copy in forward(src):
@@ -640,8 +696,13 @@
     d = ge_ref.shape[0]
     sems = scratch[-1]
     total = stat_ref[0:1, :]
-    loss_ref[0] = total[0, at_loss]
-    pairs_ref[0] = total[0, at_loss + 1]
+    sums = [
+        pltpu.make_async_copy(buf, out, sems.at[n, 0])
+        for n, (buf, out) in enumerate(zip(scratch[8:10], (loss_ref, pairs_ref)), 8)
+    ]
+    for n, copy in enumerate(sums):
+        scratch[8 + n][0] = total[0, at_loss + n]
+        copy.start()
     factor = ((1.0 - BETA_ONE) / total)[0, at_loss + 1]
     square = (1.0 - BETA_TWO) / (1.0 - BETA_ONE) ** 2
     fix_two = 1.0 / (1.0 - BETA_TWO**STEP)
@@ -663,7 +724,7 @@
         for g_ref, w_ref, one_ref, two_ref, _, bufs in tables:
 
             def rows(j, _):
-                at = pl.ds(pl.multiple_of(i * strip + j * 16, 16), 16)
+                at = pl.ds(pl.multiple_of(i * strip, 16), strip)
                 gradient = g_ref[at, :] * factor
                 weight = w_ref[at, :]
                 one = BETA_ONE * one_ref[at, :] + gradient
@@ -677,7 +738,7 @@
                 bufs[3][at, :] = new.astype(BF16)
                 return 0
 
-            lax.fori_loop(0, strip // 16, rows, 0, unroll=True)
+            rows(0, 0)
         for copy in copies(i):
             copy.start()
         return 0
@@ -687,6 +748,8 @@
     for i in range(steps):
         for copy in copies(i):
             copy.wait()
+    for copy in sums:
+        copy.wait()
 
 
 def per_device(
@@ -723,6 +786,7 @@
     smem = pl.BlockSpec(memory_space=pltpu.SMEM)
     dma = pltpu.SemaphoreType.DMA
     hbm = functools.partial(pltpu.with_memory_space_constraint, memory_space=pltpu.HBM)
+    batches = ng if ng <= 4 else 1
     scratch = [
         pltpu.VMEM((ns, cap), I32),
         pltpu.VMEM((3, segs, SEG), I32),
@@ -737,8 +801,8 @@
         pltpu.VMEM((ns, *block), F32),
         pltpu.VMEM((ke, dp), F32),
         pltpu.VMEM((kr, dp), F32),
-        pltpu.VMEM((ke, ne), BF16),
-        pltpu.VMEM((kr, nrp), BF16),
+        pltpu.VMEM((batches, ke, ne), BF16),
+        pltpu.VMEM((batches, 2 * kr, nrp), BF16),
         pltpu.VMEM((edges, ke), BF16),
         pltpu.VMEM((edges, ke), BF16),
         pltpu.VMEM((edges, 2 * kr), BF16),
@@ -770,6 +834,7 @@
         dma((ng, ns)),
         dma((ny, ns)),
         dma((max(ny - 1, 1), ns)),
+        pltpu.SemaphoreType.REGULAR,
     ]
     small = [
         requests[0],
@@ -792,7 +857,7 @@
         need += sum(padded(x) for x in held)
     operands = small + rows + (moments if keep else [])
     ge, gr, stat, *passed = pl.pallas_call(
-        functools.partial(exchange_kernel, ns, ng, (d, ne, nr, cap, edges, neg), int(keep)),
+        functools.partial(exchange_kernel, ns, ng, (d, ne, nr, cap, edges, neg), int(keep), batches > 1),
         out_shape=outs,
         in_specs=[smem] + [any_space] * len(operands),
         out_specs=[vmem] * len(outs),
@@ -813,8 +878,8 @@
         functools.partial(adamw_kernel, at_loss, strip),
         out_shape=shapes + [one, one],
         in_specs=[vmem] * 9,
-        out_specs=[any_space] * 8 + [smem, smem],
-        scratch_shapes=[pltpu.VMEM(x.shape, x.dtype) for x in shapes] + [dma((8, d // strip))],
+        out_specs=[any_space] * 10,
+        scratch_shapes=[pltpu.VMEM(x.shape, x.dtype) for x in shapes] + [pltpu.SMEM((1,), F32)] * 2 + [dma((10, d // strip))],
         compiler_params=pltpu.CompilerParams(vmem_limit_bytes=32 * 1024 * 1024),
     )(stat, ge, gr, *tables)
     e_new, e_one, e_two, e_low, r_new, r_one, r_two, r_low = (x.T for x in outs)

time: 57.1 us -> 51.3 us (0.90)
  Pallas kernels: 55.6 us -> 49.6 us
    pallas_call x1, Pallas kernels: 50.3 us -> 44.9 us  [per_device(): pl.pallas_call(functools.partial(exchange_kernel, ns, ng, (d, ne, nr, cap...]
    pallas_call x1, Pallas kernels: 5.31 us -> 4.74 us  [per_device(): pl.pallas_call(functools.partial(adamw_kernel, at_loss, strip), out_shape...]
where the time goes in v4:
time: 51.3 us; the launch traced here: 51.1 us
  Pallas kernels  49.6 us (97%)
  between operations  1.46 us (3%)
    pallas_call x1, Pallas kernels, per_device(): pl.pallas_call(functools.partial(exchange_kernel, ns, ng, (d, ne, nr, cap...  44.9 us
    pallas_call x1, Pallas kernels, per_device(): pl.pallas_call(functools.partial(adamw_kernel, at_loss, strip), out_shape...  4.74 us

profile of v4, /device:TPU:0, one launch (start us, length us, event | category | flops | bytes accessed | tf_op | source)
XLA Modules:
  0.0 51.1 jit_solution(6061340519563188606)
XLA Ops:
  1.3 44.9 %shard_map.195 = (f32[400,1024]{1,0:T(8,128)S(1)}, f32[400,784]{1,0:T(8,128)S(1)}, f32[8,128]{1,0:T(8,128)S(1)}, f32[400,1024]{1,0:T(8,128)S(1)}, f32[400,784]{1...) custom-call(s32[1]{0:T(128)S(6)} %copy.22.valid_ref, ...), custom_call_target="tpu_custom_call" | custom-call | tf_op jit(solution)/shard_map/pallas_call | solution.py:859
  46.2 4.7 %shard_map.196 = (f32[400,1024]{1,0:T(8,128)}, f32[400,1024]{1,0:T(8,128)}, f32[400,1024]{1,0:T(8,128)}, bf16[400,1024]{1,0:T(8,128)(2,1)}, f32[400,784]{1,0:T(8...) custom-call(f32[8,128]{1,0:T(8,128)S(1)} %get-tuple-element.29.stat_ref,, ...), custom_call_target="tpu_custom_call" | custom-call | tf_op jit(solution)/shard_map/pallas_call | solution.py:877

commit v5 on v4

--- a/solution.py
+++ b/solution.py
@@ -565,7 +565,7 @@
         return block_copy(group_down(dy), src, mate, core_send.at[dy, src])
 
     sequence = [0] + near
-    lag = 2
+    lag = 4
     handed = [0]
 
     def hand_over_to(end):
@@ -618,6 +618,13 @@
             ge_ref[...] = part_e
             gr_ref[...] = part_r[:, 0:nr]
 
+    def drain_sends(ks):
+        for k in ks:
+            for copy in forward(shard_at(k)):
+                copy.wait_send()
+            for dy in range(1, ny):
+                hand_over(dy, shard_at(k)).wait_send()
+
     def pass_on(idx):
         k = sequence[idx]
         if k:
@@ -651,6 +658,7 @@
     def _():
         hand_over_last()
 
+    drain_sends(sequence[:-2])
     for n in range(2 * quarter, 4 * quarter):
         add_batch(n)
 
@@ -661,12 +669,7 @@
 
     stat_ref[...] = lax.fori_loop(0, ng, stat, jnp.zeros((8, LANE), F32))
 
-    for k in sequence:
-        src = shard_from(k)
-        for copy in forward(src):
-            copy.wait_send()
-        for dy in range(1, ny):
-            hand_over(dy, src).wait_send()
+    drain_sends(sequence[-2:])
 
 
 def adamw_kernel(

time: 51.3 us -> 50.6 us (0.986)
  Pallas kernels: 49.6 us -> 48.9 us
    pallas_call x1, Pallas kernels: 44.9 us -> 44.1 us  [per_device(): pl.pallas_call(functools.partial(exchange_kernel, ns, ng, (d, ne, nr, cap...]
where the time goes in v5:
time: 50.6 us; the launch traced here: 50.3 us
  Pallas kernels  48.9 us (97%)
  between operations  1.46 us (3%)
    pallas_call x1, Pallas kernels, per_device(): pl.pallas_call(functools.partial(exchange_kernel, ns, ng, (d, ne, nr, cap...  44.1 us
    pallas_call x1, Pallas kernels, per_device(): pl.pallas_call(functools.partial(adamw_kernel, at_loss, strip), out_shape...  4.74 us

profile of v5, /device:TPU:0, one launch (start us, length us, event | category | flops | bytes accessed | tf_op | source)
XLA Modules:
  0.0 50.3 jit_solution(12858552013983151647)
XLA Ops:
  1.3 44.1 %shard_map.195 = (f32[400,1024]{1,0:T(8,128)S(1)}, f32[400,784]{1,0:T(8,128)S(1)}, f32[8,128]{1,0:T(8,128)S(1)}, f32[400,1024]{1,0:T(8,128)S(1)}, f32[400,784]{1...) custom-call(s32[1]{0:T(128)S(6)} %copy.22.valid_ref, ...), custom_call_target="tpu_custom_call" | custom-call | tf_op jit(solution)/shard_map/pallas_call | solution.py:862
  45.4 4.7 %shard_map.196 = (f32[400,1024]{1,0:T(8,128)}, f32[400,1024]{1,0:T(8,128)}, f32[400,1024]{1,0:T(8,128)}, bf16[400,1024]{1,0:T(8,128)(2,1)}, f32[400,784]{1,0:T(8...) custom-call(f32[8,128]{1,0:T(8,128)S(1)} %get-tuple-element.29.stat_ref,, ...), custom_call_target="tpu_custom_call" | custom-call | tf_op jit(solution)/shard_map/pallas_call | solution.py:880

commit v6 on v5

--- a/solution.py
+++ b/solution.py
@@ -603,20 +603,16 @@
                 r = [gbuf[grp, src, c * cap + CAP_E : (c + 1) * cap, :] for grp, src in blocks]
             else:
                 e, r = [x[0] for x in ends], [x[1] for x in ends]
-            hi, lo = halves(jnp.concatenate(e, axis=0).T[0:size, :])
-            sgt_e[put, 0:ke] = hi
-            sgt_e[put, ke : 2 * ke] = lo
-            hi, lo = halves(jnp.concatenate(r, axis=0).T[0:size, :])
-            sgt_r[put, 0:kr] = hi
-            sgt_r[put, kr : 2 * kr] = lo
-        part_e = mm(sgt_e[:, 0:ke], oh_e[at]) + mm(sgt_e[:, ke : 2 * ke], oh_e[at])
-        part_r = mm(sgt_r[...], oh_r[at])
-        if n:
-            ge_ref[...] += part_e
-            gr_ref[...] += part_r[:, 0:nr]
-        else:
-            ge_ref[...] = part_e
-            gr_ref[...] = part_r[:, 0:nr]
+            terms = jnp.concatenate(halves(jnp.concatenate(e, axis=0).T[0:size, :]), axis=0)
+            sums_e = mm(terms, oh_e[at])
+            terms = jnp.concatenate(halves(jnp.concatenate(r, axis=0).T[0:size, :]), axis=1)
+            sums_r = mm(terms, oh_r[at])
+            if n:
+                ge_ref[put, :] += sums_e[0:size] + sums_e[size:]
+                gr_ref[put, :] += sums_r[:, 0:nr]
+            else:
+                ge_ref[put, :] = sums_e[0:size] + sums_e[size:]
+                gr_ref[put, :] = sums_r[:, 0:nr]
 
     def drain_sends(ks):
         for k in ks:

time: 50.6 us -> 50.7 us (level)
  no operation moved by 1% of the time
where the time goes in v6:
time: 50.7 us; the launch traced here: 50.4 us
  Pallas kernels  48.9 us (96%)
  between operations  1.46 us (3%)
    pallas_call x1, Pallas kernels, per_device(): pl.pallas_call(functools.partial(exchange_kernel, ns, ng, (d, ne, nr, cap...  44.2 us
    pallas_call x1, Pallas kernels, per_device(): pl.pallas_call(functools.partial(adamw_kernel, at_loss, strip), out_shape...  4.74 us

profile of v6, /device:TPU:0, one launch (start us, length us, event | category | flops | bytes accessed | tf_op | source)
XLA Modules:
  0.0 50.4 jit_solution(17398947516670890267)
XLA Ops:
  1.3 44.2 %shard_map.195 = (f32[400,1024]{1,0:T(8,128)S(1)}, f32[400,784]{1,0:T(8,128)S(1)}, f32[8,128]{1,0:T(8,128)S(1)}, f32[400,1024]{1,0:T(8,128)S(1)}, f32[400,784]{1...) custom-call(s32[1]{0:T(128)S(6)} %copy.22.valid_ref, ...), custom_call_target="tpu_custom_call" | custom-call | tf_op jit(solution)/shard_map/pallas_call | solution.py:858
  45.5 4.7 %shard_map.196 = (f32[400,1024]{1,0:T(8,128)}, f32[400,1024]{1,0:T(8,128)}, f32[400,1024]{1,0:T(8,128)}, bf16[400,1024]{1,0:T(8,128)(2,1)}, f32[400,784]{1,0:T(8...) custom-call(f32[8,128]{1,0:T(8,128)S(1)} %get-tuple-element.29.stat_ref,, ...), custom_call_target="tpu_custom_call" | custom-call | tf_op jit(solution)/shard_map/pallas_call | solution.py:876
